TPU v7x, 32 devices: a whole 2x2x4 slice. The times are simulated.
32 devices in a mesh: slab: 8 (over z, y), chan: 4 (over x, core).
Axes of the slice: x: 2, y: 2, z: 4, core: 2. Of those that a mesh axis runs over, the one named last changes fastest.
Arguments:
- field: bfloat16 [32, 256, 256, 256], P('chan', 'slab'), may hold values from -6 to 6
- forcing: bfloat16 [256, 256, 256], P('slab', 'chan'), may hold values from -6 to 6
- slot_column: int32 [8, 256], replicated, may hold values from -1 to 1023, as said below
- w_spec: bfloat16 [2, 32, 32, 32768], P(None, 'chan', None, 'slab'), may hold values from -12 to 12
- skip_gain: float32 [32], P('chan'), may hold values from 0.5 to 1.5
- bias: float32 [32], P('chan'), may hold values from -3 to 3
Outputs:
- output: bfloat16 [32, 256, 256, 256], P('chan', 'slab')
- gradient: bfloat16 [32, 256, 256, 256], P('chan', 'slab')
Inputs may be any that keep to these rules, and one draw needn't show every extreme that they name: `slot_column`: every kept pair index 0 to 1023 appears exactly once in the table; empty slots hold -1; the busiest slab device fills all 256 of its slots.
All inputs are finite; a program needn't handle non-finite values.
Results may differ from a plain program's by a relative error of at most 0.022.
Values may be sent and summed in bfloat16 or wider, within the bound.
No kernel may reach another device: no remote copies, remote signals or barrier semaphores. Data moves between devices by JAX's collectives and lax.ppermute only.
A program may use at most 256 MiB of HBM per device.

v0:
```python
import functools
import math

import jax
import jax.numpy as jnp
import ml_dtypes
import numpy as np
from jax import lax
from jax.experimental import pallas as pl
from jax.experimental.pallas import tpu as pltpu
from jax.sharding import PartitionSpec as P

KXY = 32
KZ = 16
ZB = 4
HALF = ZB * KXY
C1 = math.sqrt(2.0 / math.pi)
C2 = 0.044715
F32 = jnp.float32
BF16 = jnp.bfloat16
SLOTS = 128
SMALL = 16 * 2**20
LARGE = 54 * 2**20


def dot(a, b):
    return jnp.dot(a, b, preferred_element_type=F32)


def angles(freqs, count, grid_len):
    turns = (freqs[:, None] * np.arange(count)[None, :]) % grid_len
    return turns * (2.0 * math.pi / grid_len)


def half_width(table):
    return table.astype(ml_dtypes.bfloat16)


def plane_tables(grid_len):
    angle = angles(np.arange(KXY) - KXY // 2, grid_len, grid_len)
    cosine, sine = np.cos(angle), np.sin(angle)
    rows = np.zeros((ZB, grid_len, 2, ZB, KXY))
    for i in range(ZB):
        rows[i, :, 0, i, :] = cosine.T
        rows[i, :, 1, i, :] = -sine.T
    rows = rows.reshape(ZB, grid_len, 2 * HALF)
    return rows, np.concatenate([cosine, sine], 0)


def depth_tables(planes, grid_len):
    angle = angles(np.arange(KZ), planes, grid_len)
    cosine, sine = np.cos(angle), np.sin(angle)
    table = np.zeros((planes // ZB, 2, ZB, KXY, 2, KZ, KXY))
    for b in range(planes // ZB):
        for i in range(ZB):
            for j in range(KXY):
                table[b, 0, i, j, 0, :, j] = cosine[:, b * ZB + i]
                table[b, 1, i, j, 0, :, j] = sine[:, b * ZB + i]
                table[b, 0, i, j, 1, :, j] = -sine[:, b * ZB + i]
                table[b, 1, i, j, 1, :, j] = cosine[:, b * ZB + i]
    return table.reshape(planes // ZB, 2 * HALF, 2 * KZ * KXY)


def spread_table():
    return np.repeat(np.eye(SLOTS), KZ, axis=1)


def whole(array):
    return pl.BlockSpec(array.shape, lambda *_: (0,) * len(array.shape))


def scalars():
    return pl.BlockSpec(memory_space=pltpu.SMEM)


def column_sums(u_ref, rt_ref, p_ref, first, last):
    rows = slice(first * 2 * KXY, last * 2 * KXY)
    total = dot(u_ref[0, rows], rt_ref[0])
    for i in range(1, ZB):
        total += dot(u_ref[i, rows], rt_ref[i])
    total = total.reshape(last - first, 2 * KXY, 2 * HALF)
    low, high = total[:, :KXY], total[:, KXY:]
    real = low[:, :, :HALF] + high[:, :, HALF:]
    imag = low[:, :, HALF:] - high[:, :, :HALF]
    rows = slice(first * KXY, last * KXY)
    p_ref[rows, :HALF] = real.reshape(-1, HALF).astype(BF16)
    p_ref[rows, HALF:] = imag.reshape(-1, HALF).astype(BF16)


def store_turned(total, ph_ref, out_ref, factor):
    half = KZ * KXY
    cosine, sine = ph_ref[0:1, :], ph_ref[1:2, :]
    real, imag = total[:, :half], total[:, half:]
    out_ref[:, :half] = ((real * cosine + imag * sine) * factor).astype(BF16)
    out_ref[:, half:] = ((imag * cosine - real * sine) * factor).astype(BF16)


def turn_spectra(q_ref, ph_ref, turned_ref):
    half = KZ * KXY
    cosine, sine = ph_ref[0:1, :], ph_ref[1:2, :]
    real, imag = q_ref[:, :half].astype(F32), q_ref[:, half:].astype(F32)
    turned_ref[:, :half] = (real * cosine - imag * sine).astype(BF16)
    turned_ref[:, half:] = (real * sine + imag * cosine).astype(BF16)


def resident():
    return pl.BlockSpec(memory_space=pltpu.VMEM)


def anywhere():
    return pl.BlockSpec(memory_space=pltpu.HBM)


def column_fields(zz_ref, txt, c):
    low = zz_ref[c * KXY : (c + 1) * KXY, :]
    high = jnp.concatenate([-low[:, HALF:], low[:, :HALF]], 1)
    return dot(txt, jnp.concatenate([low, high], 0)).astype(BF16)


def plane_rows(u_ref, tx, c, i, plane):
    u_ref[i, c * 2 * KXY : (c + 1) * 2 * KXY, :] = dot(tx, plane).astype(BF16)


def fetch_block(v_ref, kept_ref, sems, b):
    slot = lax.rem(b, kept_ref.shape[0])
    return pltpu.make_async_copy(v_ref.at[:, pl.ds(b * ZB, ZB)], kept_ref.at[slot], sems.at[slot])


def fetch_table(hbm_ref, table_ref, sems, b):
    slot = lax.rem(b, table_ref.shape[0])
    return pltpu.make_async_copy(hbm_ref.at[b], table_ref.at[slot], sems.at[slot])


def analyse_kernel(
    factor, v_ref, rt_ref, tx_ref, tz_hbm, ph_ref, out_ref, acc_ref, p_ref, u_ref, kept_ref, tz_ref, sems, tz_sems
):
    channels, planes = v_ref.shape[:2]
    blocks = planes // ZB
    half = channels // 2
    ahead = kept_ref.shape[0] - 1
    for b in range(ahead):
        fetch_block(v_ref, kept_ref, sems, b).start()
        fetch_table(tz_hbm, tz_ref, tz_sems, b).start()
    tx = tx_ref[...]
    acc_ref[...] = jnp.zeros_like(acc_ref)

    def body(b, carry):
        @pl.when(b + ahead < blocks)
        def _():
            fetch_block(v_ref, kept_ref, sems, b + ahead).start()
            fetch_table(tz_hbm, tz_ref, tz_sems, b + ahead).start()

        fetch_block(v_ref, kept_ref, sems, b).wait()
        slot = lax.rem(b, ahead + 1)
        for c in range(channels):
            for i in range(ZB):
                plane_rows(u_ref, tx, c, i, kept_ref[slot, c, i])
            if c == channels - 2:
                column_sums(u_ref, rt_ref, p_ref, 0, half)
        column_sums(u_ref, rt_ref, p_ref, half, channels)
        fetch_table(tz_hbm, tz_ref, tz_sems, b).wait()
        acc_ref[...] += dot(p_ref[...], tz_ref[slot])
        return carry

    lax.fori_loop(0, blocks, body, 0)
    store_turned(acc_ref[...], ph_ref, out_ref, factor)


def analyse(volume, rt, tx, tz, phase, factor):
    channels, planes, rows, grid_len = volume.shape
    width = 2 * KZ * KXY
    return pl.pallas_call(
        functools.partial(analyse_kernel, factor),
        in_specs=[anywhere(), resident(), resident(), anywhere(), resident()],
        out_specs=resident(),
        out_shape=jax.ShapeDtypeStruct((channels * KXY, width), BF16),
        scratch_shapes=[
            pltpu.VMEM((channels * KXY, width), F32),
            pltpu.VMEM((channels * KXY, 2 * HALF), BF16),
            pltpu.VMEM((ZB, channels * 2 * KXY, grid_len), BF16),
            pltpu.VMEM((3, channels, ZB, rows, grid_len), BF16),
            pltpu.VMEM((3,) + tz.shape[1:], BF16),
            pltpu.SemaphoreType.DMA((3,)),
            pltpu.SemaphoreType.DMA((3,)),
        ],
        compiler_params=pltpu.CompilerParams(vmem_limit_bytes=LARGE),
        cost_estimate=pl.CostEstimate(
            flops=512 * volume.size, bytes_accessed=2 * volume.size, transcendentals=0
        ),
        name="analyse",
    )(volume, rt, tx, tz, phase)


def forced_kernel(factor, v_ref, rt_ref, tx_ref, tz_hbm, ph_ref, out_ref, p_ref, u_ref, tz_ref, sem):
    tx = tx_ref[...]
    copy = pltpu.make_async_copy(tz_hbm, tz_ref, sem)
    copy.start()
    blocks = v_ref.shape[0] // ZB
    for b in range(blocks):
        for i in range(ZB):
            plane_rows(u_ref, tx, b, i, v_ref[b * ZB + i])
    column_sums(u_ref, rt_ref, p_ref, 0, blocks)
    copy.wait()
    total = dot(p_ref[:KXY], tz_ref[0])
    for b in range(1, blocks):
        total += dot(p_ref[b * KXY : (b + 1) * KXY], tz_ref[b])
    store_turned(total, ph_ref, out_ref, factor)


def analyse_forced(forcing, rt, tx, tz, phase, factor):
    planes, _, grid_len = forcing.shape
    blocks = planes // ZB
    return pl.pallas_call(
        functools.partial(forced_kernel, factor),
        in_specs=[resident(), resident(), resident(), anywhere(), resident()],
        out_shape=jax.ShapeDtypeStruct((KXY, 2 * KZ * KXY), BF16),
        scratch_shapes=[
            pltpu.VMEM((blocks * KXY, 2 * HALF), BF16),
            pltpu.VMEM((ZB, blocks * 2 * KXY, grid_len), BF16),
            pltpu.VMEM(tz.shape, BF16),
            pltpu.SemaphoreType.DMA,
        ],
        compiler_params=pltpu.CompilerParams(vmem_limit_bytes=SMALL),
        name="forced",
    )(forcing, rt, tx, tz, phase)


def gelu_planes(field, coefs_ref, c):
    cubic, linear, half, square = (coefs_ref[c, k].astype(BF16) for k in range(4))
    squared = field * field
    inner = field * (squared * cubic + linear)
    tangent = jnp.tanh(inner.astype(F32))
    upper = (1.0 + tangent).astype(BF16)
    lower = (1.0 - tangent).astype(BF16)
    value = field * (upper * half)
    slope = upper + value * lower * (squared * square + BF16(2.0 * C1))
    return value, value * slope


def send_block(buf_ref, o_ref, sems, b):
    slot = lax.rem(b, 2)
    return pltpu.make_async_copy(buf_ref.at[slot], o_ref.at[:, pl.ds(b * ZB, ZB)], sems.at[slot])


def fetch_forced(f_refs, raw_ref, sems, b, slot):
    return [
        pltpu.make_async_copy(ref.at[pl.ds(b * ZB, ZB)], raw_ref.at[slot, k], sems.at[slot, k])
        for k, ref in enumerate(f_refs)
    ]


def middle_kernel(factor, parts, *refs):
    q_ref, v_ref = refs[:2]
    f_refs = refs[2 : 2 + parts]
    (place_ref, coefs_ref, scale_ref, shift_ref, rt_ref, bd_ref, tx_ref, txt_ref, tz_hbm, ts_hbm, ph_ref) = refs[
        2 + parts : 13 + parts
    ]
    (o_ref, g_ref, back_ref, acc_ref, p_ref, u_ref, zz_ref, turned_ref, x_ref, f_ref, even_ref, odd_ref) = refs[
        13 + parts : 25 + parts
    ]
    kept_ref, buf_ref, grad_ref, raw_ref, tz_ref, ts_ref = refs[25 + parts : 31 + parts]
    out_sems, grad_sems, in_sems, v_sems, tz_sems, ts_sems = refs[31 + parts :]
    channels, planes = v_ref.shape[:2]
    blocks = planes // ZB
    half = channels // 2
    rows = raw_ref.shape[3]
    for copy in fetch_forced(f_refs, raw_ref, in_sems, 0, 0):
        copy.start()
    fetch_table(ts_hbm, ts_ref, ts_sems, 0).start()
    fetch_block(v_ref, kept_ref, v_sems, 0).start()
    fetch_table(tz_hbm, tz_ref, tz_sems, 0).start()
    turn_spectra(q_ref, ph_ref, turned_ref)
    acc_ref[...] = jnp.zeros_like(acc_ref)
    tx, txt = tx_ref[...], txt_ref[...]
    grads = (even_ref, odd_ref)

    def spatial(c, i):
        return dot(x_ref[c], bd_ref[i]).astype(BF16)

    def body(b, carry):
        slot = lax.rem(b, 2)

        @pl.when(b + 1 < blocks)
        def _():
            for copy in fetch_forced(f_refs, raw_ref, in_sems, b + 1, 1 - slot):
                copy.start()
            fetch_table(ts_hbm, ts_ref, ts_sems, b + 1).start()
            fetch_block(v_ref, kept_ref, v_sems, b + 1).start()
            fetch_table(tz_hbm, tz_ref, tz_sems, b + 1).start()

        for copy in fetch_forced(f_refs, raw_ref, in_sems, b, slot):
            copy.wait()
        fetch_table(ts_hbm, ts_ref, ts_sems, b).wait()
        fetch_block(v_ref, kept_ref, v_sems, b).wait()
        fetch_table(tz_hbm, tz_ref, tz_sems, b).wait()

        @pl.when(b > 1)
        def _():
            send_block(buf_ref, o_ref, out_sems, b - 2).wait()
            send_block(grad_ref, g_ref, grad_sems, b - 2).wait()

        for k in range(parts):
            f_ref[:, pl.ds(pl.multiple_of(place_ref[k] * rows, rows), rows), :] = raw_ref[slot, k]
        zz_ref[...] = (dot(turned_ref[...], ts_ref[slot]) * scale_ref[...] + shift_ref[...]).astype(BF16)
        for c in range(channels):
            x_ref[c] = column_fields(zz_ref, txt, c)
        for c in range(channels):
            ahead = spatial(c, 0)
            for i in range(ZB):
                here = ahead
                if i < ZB - 1:
                    ahead = spatial(c, i + 1)
                if c > 0:
                    plane_rows(u_ref, tx, c - 1, i, grads[(c - 1) % 2][i])
                value, grad = gelu_planes(here + (kept_ref[slot, c, i] + f_ref[i]), coefs_ref, c)
                buf_ref[slot, c, i] = value
                grad_ref[slot, c, i] = grad
                grads[c % 2][i] = grad
            if c == channels - 1:
                column_sums(u_ref, rt_ref, p_ref, 0, half)
        for i in range(ZB):
            plane_rows(u_ref, tx, channels - 1, i, grads[(channels - 1) % 2][i])
        column_sums(u_ref, rt_ref, p_ref, half, channels)
        acc_ref[...] += dot(p_ref[...], tz_ref[slot])
        send_block(buf_ref, o_ref, out_sems, b).start()
        send_block(grad_ref, g_ref, grad_sems, b).start()
        return carry

    lax.fori_loop(0, blocks, body, 0)
    store_turned(acc_ref[...], ph_ref, back_ref, factor)
    for b in (blocks - 2, blocks - 1):
        send_block(buf_ref, o_ref, out_sems, b).wait()
        send_block(grad_ref, g_ref, grad_sems, b).wait()


def middle(spectra, kept, forced, place, coefs, scale, shift, rt, bd, tx, txt, tz, ts, phase, factor):
    channels, planes, rows, grid_len = kept.shape
    width = 2 * KZ * KXY
    parts = len(forced)
    return pl.pallas_call(
        functools.partial(middle_kernel, factor, parts),
        in_specs=[resident(), anywhere()] + [anywhere()] * parts + [scalars()] * 2 + [resident()] * 6 + [anywhere()] * 2 + [resident()],
        out_specs=[anywhere(), anywhere(), resident()],
        out_shape=[
            jax.ShapeDtypeStruct(kept.shape, BF16),
            jax.ShapeDtypeStruct(kept.shape, BF16),
            jax.ShapeDtypeStruct((channels * KXY, width), BF16),
        ],
        scratch_shapes=[
            pltpu.VMEM((channels * KXY, width), F32),
            pltpu.VMEM((channels * KXY, 2 * HALF), BF16),
            pltpu.VMEM((ZB, channels * 2 * KXY, grid_len), BF16),
            pltpu.VMEM((channels * KXY, 2 * HALF), BF16),
            pltpu.VMEM((channels * KXY, width), BF16),
            pltpu.VMEM((channels, rows, 2 * HALF), BF16),
            pltpu.VMEM((ZB, rows, grid_len), BF16),
            pltpu.VMEM((ZB, rows, grid_len), BF16),
            pltpu.VMEM((ZB, rows, grid_len), BF16),
            pltpu.VMEM((2, channels, ZB, rows, grid_len), BF16),
            pltpu.VMEM((2, channels, ZB, rows, grid_len), BF16),
            pltpu.VMEM((2, channels, ZB, rows, grid_len), BF16),
            pltpu.VMEM((2, parts, ZB) + forced[0].shape[1:], BF16),
            pltpu.VMEM((2,) + tz.shape[1:], BF16),
            pltpu.VMEM((2,) + ts.shape[1:], BF16),
            pltpu.SemaphoreType.DMA((2,)),
            pltpu.SemaphoreType.DMA((2,)),
            pltpu.SemaphoreType.DMA((2, parts)),
            pltpu.SemaphoreType.DMA((2,)),
            pltpu.SemaphoreType.DMA((2,)),
            pltpu.SemaphoreType.DMA((2,)),
        ],
        compiler_params=pltpu.CompilerParams(vmem_limit_bytes=LARGE),
        cost_estimate=pl.CostEstimate(
            flops=1024 * kept.size, bytes_accessed=2 * kept.size, transcendentals=kept.size
        ),
        name="middle",
    )(spectra, kept, *forced, place, coefs, scale, shift, rt, bd, tx, txt, tz, ts, phase)


def finish_kernel(
    q_ref, g_ref, gain_ref, bd_ref, txt_ref, ts_hbm, ph_ref, o_ref, zz_ref, turned_ref, x_ref, kept_ref, buf_ref, ts_ref,
    sems, in_sems, ts_sems,
):
    channels, planes = g_ref.shape[:2]
    blocks = planes // ZB
    ahead = kept_ref.shape[0] - 1
    for b in range(ahead):
        fetch_table(ts_hbm, ts_ref, ts_sems, b).start()
        fetch_block(g_ref, kept_ref, in_sems, b).start()
    turn_spectra(q_ref, ph_ref, turned_ref)
    txt = txt_ref[...]

    def body(b, carry):
        @pl.when(b + ahead < blocks)
        def _():
            fetch_table(ts_hbm, ts_ref, ts_sems, b + ahead).start()
            fetch_block(g_ref, kept_ref, in_sems, b + ahead).start()

        slot = lax.rem(b, ahead + 1)
        fetch_table(ts_hbm, ts_ref, ts_sems, b).wait()
        fetch_block(g_ref, kept_ref, in_sems, b).wait()

        @pl.when(b > 1)
        def _():
            send_block(buf_ref, o_ref, sems, b - 2).wait()

        zz_ref[...] = dot(turned_ref[...], ts_ref[slot]).astype(BF16)
        for c in range(channels):
            x_ref[c] = column_fields(zz_ref, txt, c)
        for c in range(channels):
            for i in range(ZB):
                plane = kept_ref[slot, c, i].astype(F32)
                buf_ref[lax.rem(b, 2), c, i] = (dot(x_ref[c], bd_ref[i]) + gain_ref[c] * plane).astype(BF16)
        send_block(buf_ref, o_ref, sems, b).start()
        return carry

    lax.fori_loop(0, blocks, body, 0)
    for b in (blocks - 2, blocks - 1):
        send_block(buf_ref, o_ref, sems, b).wait()


def finish(spectra, grads, gain, bd, txt, ts, phase):
    channels, planes, rows, grid_len = grads.shape
    width = 2 * KZ * KXY
    return pl.pallas_call(
        finish_kernel,
        in_specs=[resident(), anywhere(), scalars(), resident(), resident(), anywhere(), resident()],
        out_specs=anywhere(),
        out_shape=jax.ShapeDtypeStruct(grads.shape, BF16),
        scratch_shapes=[
            pltpu.VMEM((channels * KXY, 2 * HALF), BF16),
            pltpu.VMEM((channels * KXY, width), BF16),
            pltpu.VMEM((channels, rows, 2 * HALF), BF16),
            pltpu.VMEM((3, channels, ZB, rows, grid_len), BF16),
            pltpu.VMEM((2, channels, ZB, rows, grid_len), BF16),
            pltpu.VMEM((3,) + ts.shape[1:], BF16),
            pltpu.SemaphoreType.DMA((2,)),
            pltpu.SemaphoreType.DMA((3,)),
            pltpu.SemaphoreType.DMA((3,)),
        ],
        compiler_params=pltpu.CompilerParams(vmem_limit_bytes=LARGE),
        cost_estimate=pl.CostEstimate(
            flops=512 * grads.size, bytes_accessed=2 * grads.size, transcendentals=0
        ),
        name="finish",
    )(spectra, grads, gain, bd, txt, ts, phase)


def depth_mask(lanes):
    depth = lax.broadcasted_iota(jnp.int32, (KZ, 1, lanes), 0)
    lane = lax.broadcasted_iota(jnp.int32, (KZ, 1, lanes), 2)
    return (lane % KZ == depth).astype(F32)


def spread(sums, table, mask, channels):
    out = dot(sums, table)
    out = out.reshape(2, KZ, channels, out.shape[-1]) * mask[None]
    return jnp.sum(out, axis=1)


def gather_depth(values, table_t, mask):
    parts, channels, lanes = values.shape
    out = (values[:, None] * mask[None]).reshape(parts * KZ * channels, lanes)
    return dot(out.astype(BF16), table_t)


LANES = 512
GROUP = 8
WIDE = GROUP * KXY


def iota(shape, axis):
    return lax.broadcasted_iota(jnp.int32, shape, axis)


def one_hot(hit):
    return jnp.where(hit, 1.0, 0.0).astype(BF16)


def row_order(channels):
    shape = (WIDE, channels * KXY)
    row, lane = iota(shape, 0), iota(shape, 1)
    return one_hot((row // GROUP == lane % KXY) & (row % GROUP == lane // KXY))


def row_order_back(channels):
    shape = (channels * KXY, WIDE)
    row, lane = iota(shape, 0), iota(shape, 1)
    return one_hot((lane // GROUP == row % KXY) & (lane % GROUP == row // KXY))


def chosen(slots_ref, k, columns):
    capacity = slots_ref.shape[-1]
    return one_hot(iota((columns, capacity), 0) == slots_ref[k])


def own_lanes():
    shape = (GROUP, 1, WIDE)
    return (iota(shape, 0) == iota(shape, 2) // KXY).astype(F32)


def to_slots_kernel(slots_ref, d_ref, *refs):
    others, (o_ref, t_ref) = refs[:-2], refs[-2:]
    channels = d_ref.shape[0] // KXY
    data = d_ref[...]
    if others:
        extra = others[0][...].astype(F32)
        for other in others[1:]:
            extra += other[...].astype(F32)
        data = data.astype(F32).reshape(channels, KXY, -1) + extra[None]
        data = data.reshape(channels * KXY, -1).astype(BF16)
    data = dot(row_order(channels), data).astype(BF16)
    row, lane = iota((WIDE, WIDE), 0), iota((WIDE, WIDE), 1)
    same = row % KXY == lane % KXY
    mask = own_lanes()
    groups = KXY // GROUP
    for m in range(GROUP):
        pick = one_hot(same & (row // KXY == m))
        for k in range(2 * KZ // GROUP):
            out = dot(data[:, k * WIDE : (k + 1) * WIDE], pick)
            out = jnp.sum(out.reshape(groups, GROUP, GROUP, WIDE) * mask[None], axis=1)
            first = (k * GROUP + m) * GROUP
            for g in range(groups):
                t_ref[first : first + GROUP, g * WIDE : (g + 1) * WIDE] = out[g]
    table = t_ref[...].astype(BF16)
    if channels < GROUP:
        shape = (2 * KZ * channels, WIDE)
        row, lane = iota(shape, 0), iota(shape, 1)
        keep = (row // channels == lane // GROUP) & (row % channels == lane % GROUP)
        table = dot(one_hot(keep), table).astype(BF16)
    for k in range(slots_ref.shape[0]):
        o_ref[k] = dot(table, chosen(slots_ref, k, KXY * KXY)).astype(BF16)


def to_slots(slots, coefs, others):
    slabs, _, capacity = slots.shape
    return pl.pallas_call(
        to_slots_kernel,
        out_shape=jax.ShapeDtypeStruct((slabs, coefs.shape[0], capacity), BF16),
        scratch_shapes=[pltpu.VMEM((WIDE, KXY * KXY), F32)],
        compiler_params=pltpu.CompilerParams(vmem_limit_bytes=SMALL),
        name="to_slots",
    )(slots, coefs, *others)


def to_columns_kernel(places, slots_ref, *refs):
    (a_refs, b_refs), (o_ref, t_ref) = (refs[:2], refs[2:4]), refs[4:]
    channels = o_ref.shape[0] // KXY
    columns = KXY * KXY
    half = slots_ref.shape[0] // 2

    def piece(pair, k):
        return pair[k // half][k % half]

    total = None
    for k, place in enumerate(places):
        both = jnp.concatenate([piece(a_refs, k), piece(b_refs, place)], 0)
        part = lax.dot_general(
            both, chosen(slots_ref, k, columns), (((1,), (1,)), ((), ())), preferred_element_type=F32
        )
        total = part if total is None else total + part
    if channels < GROUP:
        shape = (WIDE, 2 * KZ * channels)
        row, lane = iota(shape, 0), iota(shape, 1)
        keep = (lane // channels == row // GROUP) & (lane % channels == row % GROUP)
        total = dot(one_hot(keep), total.astype(BF16))
    t_ref[...] = total
    row, lane = iota((WIDE, WIDE), 0), iota((WIDE, WIDE), 1)
    same = row % KXY == lane % KXY
    mask = own_lanes()
    groups = KXY // GROUP
    back = row_order_back(channels)
    picks = [one_hot(same & (lane // KXY == m)) for m in range(GROUP)]
    for k in range(2 * KZ // GROUP):
        found = None
        for m in range(GROUP):
            first = (k * GROUP + m) * GROUP
            rows = t_ref[first : first + GROUP, :]
            parts = [(rows[None, :, g * WIDE : (g + 1) * WIDE] * mask).reshape(WIDE // groups, WIDE) for g in range(groups)]
            part = dot(jnp.concatenate(parts, 0).astype(BF16), picks[m])
            found = part if found is None else found + part
        o_ref[:, k * WIDE : (k + 1) * WIDE] = dot(back, found.astype(BF16)).astype(BF16)


def to_columns(slots, pieces, places, channels):
    return pl.pallas_call(
        functools.partial(to_columns_kernel, places),
        out_shape=jax.ShapeDtypeStruct((channels * KXY, 2 * KZ * KXY), BF16),
        scratch_shapes=[pltpu.VMEM((WIDE, KXY * KXY), F32)],
        compiler_params=pltpu.CompilerParams(vmem_limit_bytes=SMALL),
        name="to_columns",
    )(slots, *pieces)


def fetch_lanes(hbm_ref, w_ref, sems, k):
    lanes = pl.ds(k * LANES, LANES)
    return pltpu.make_async_copy(hbm_ref.at[:, :, :, lanes], w_ref.at[:, :, :, lanes], sems.at[k])


def mix_kernel(groups, p_ref, w_hbm, e_ref, o_ref, s_ref, w_ref, sems):
    channels, outs, length = w_ref.shape[1:]
    for k in range(length // LANES):
        fetch_lanes(w_hbm, w_ref, sems, k).start()
    own = outs // groups
    mask = depth_mask(LANES)
    per = SLOTS * KZ // LANES
    total = p_ref[0].astype(F32)
    for k in range(1, p_ref.shape[0]):
        total += p_ref[k].astype(F32)
    s_ref[...] = total.astype(BF16)

    def body(k, carry):
        slot = pl.multiple_of(k // per * SLOTS, SLOTS)
        part = pl.multiple_of(k % per * LANES, LANES)
        lane = pl.multiple_of(k * LANES, LANES)
        fetch_lanes(w_hbm, w_ref, sems, k).wait()
        u = spread(s_ref[:, pl.ds(slot, SLOTS)], e_ref[:, pl.ds(part, LANES)], mask, channels)
        real = jnp.zeros((outs, LANES), F32)
        imag = jnp.zeros((outs, LANES), F32)
        for c in range(channels):
            w0 = w_ref[0, c, :, pl.ds(lane, LANES)].astype(F32)
            w1 = w_ref[1, c, :, pl.ds(lane, LANES)].astype(F32)
            ur, ui = u[0, c : c + 1], u[1, c : c + 1]
            real += w0 * ur - w1 * ui
            imag += w1 * ur + w0 * ui
        for g in range(groups):
            o_ref[g, 0, :, pl.ds(lane, LANES)] = real[g * own : (g + 1) * own].astype(BF16)
            o_ref[g, 1, :, pl.ds(lane, LANES)] = imag[g * own : (g + 1) * own].astype(BF16)
        return carry

    lax.fori_loop(0, length // LANES, body, 0)


def mix(sums, weights, table, groups):
    _, channels, outs, length = weights.shape
    return pl.pallas_call(
        functools.partial(mix_kernel, groups),
        out_shape=jax.ShapeDtypeStruct((groups, 2, outs // groups, length), BF16),
        in_specs=[resident(), anywhere(), resident()],
        scratch_shapes=[
            pltpu.VMEM(sums.shape[1:], BF16),
            pltpu.VMEM(weights.shape, BF16),
            pltpu.SemaphoreType.DMA((length // LANES,)),
        ],
        compiler_params=pltpu.CompilerParams(vmem_limit_bytes=SMALL),
        cost_estimate=pl.CostEstimate(
            flops=4 * weights.size, bytes_accessed=2 * weights.size, transcendentals=0
        ),
        name="mix",
    )(sums, weights, table)


def compress_kernel(a_ref, b_ref, et_ref, o_ref):
    width = SLOTS * KZ
    mask = depth_mask(width)
    lane = lax.broadcasted_iota(jnp.int32, (1, 1, width), 2)
    twice = jnp.where(lane % KZ == 0, 1.0, 2.0).astype(F32)
    for k in range(a_ref.shape[-1] // width):
        lanes = slice(k * width, (k + 1) * width)
        total = a_ref[:, :, lanes].astype(F32) + b_ref[:, :, lanes].astype(F32)
        out = gather_depth(total * twice, et_ref[...], mask)
        o_ref[:, k * SLOTS : (k + 1) * SLOTS] = out.astype(BF16)


def compress(kept, got, table_t):
    _, channels, length = kept.shape
    return pl.pallas_call(
        compress_kernel,
        out_shape=jax.ShapeDtypeStruct((2 * KZ * channels, length // KZ), BF16),
        compiler_params=pltpu.CompilerParams(vmem_limit_bytes=SMALL),
        name="compress",
    )(kept, got, table_t)


def unmix_kernel(s_ref, w_hbm, e_ref, et_ref, o_ref, adj_ref, w_ref, sems):
    channels, outs, length = w_ref.shape[1:]
    for k in range(length // LANES):
        fetch_lanes(w_hbm, w_ref, sems, k).start()
    groups = s_ref.shape[0]
    mask = depth_mask(LANES)
    per = SLOTS * KZ // LANES
    wide = depth_mask(SLOTS * KZ)

    def chunk(k, carry):
        def body(j, inner):
            slot = pl.multiple_of(k * SLOTS, SLOTS)
            part = pl.multiple_of(j * LANES, LANES)
            lane = pl.multiple_of(k * SLOTS * KZ + j * LANES, LANES)
            fetch_lanes(w_hbm, w_ref, sems, k * per + j).wait()
            table = e_ref[:, pl.ds(part, LANES)]
            pieces = [spread(s_ref[g, :, pl.ds(slot, SLOTS)], table, mask, outs // groups) for g in range(groups)]
            gr = jnp.concatenate([piece[0] for piece in pieces], 0)
            gi = jnp.concatenate([piece[1] for piece in pieces], 0)
            for c in range(channels):
                w0 = w_ref[0, c, :, pl.ds(lane, LANES)].astype(F32)
                w1 = w_ref[1, c, :, pl.ds(lane, LANES)].astype(F32)
                adj_ref[0, c : c + 1, pl.ds(part, LANES)] = jnp.sum(w0 * gr + w1 * gi, axis=0, keepdims=True)
                adj_ref[1, c : c + 1, pl.ds(part, LANES)] = jnp.sum(w0 * gi - w1 * gr, axis=0, keepdims=True)
            return inner

        lax.fori_loop(0, per, body, 0)
        out = gather_depth(adj_ref[...], et_ref[...], wide)
        o_ref[:, pl.ds(pl.multiple_of(k * SLOTS, SLOTS), SLOTS)] = out.astype(BF16)
        return carry

    lax.fori_loop(0, length // (SLOTS * KZ), chunk, 0)


def unmix(sums, weights, table, table_t):
    _, channels, outs, length = weights.shape
    return pl.pallas_call(
        unmix_kernel,
        out_shape=jax.ShapeDtypeStruct((2 * KZ * channels, length // KZ), BF16),
        in_specs=[resident(), anywhere(), resident(), resident()],
        scratch_shapes=[
            pltpu.VMEM((2, channels, SLOTS * KZ), F32),
            pltpu.VMEM(weights.shape, BF16),
            pltpu.SemaphoreType.DMA((length // LANES,)),
        ],
        compiler_params=pltpu.CompilerParams(vmem_limit_bytes=SMALL),
        cost_estimate=pl.CostEstimate(
            flops=4 * weights.size, bytes_accessed=2 * weights.size, transcendentals=0
        ),
        name="unmix",
    )(sums, weights, table, table_t)


def bits_of(count):
    return tuple(1 << k for k in reversed(range(count.bit_length() - 1)))


def offsets(route):
    found = [0]
    for bit in route:
        found = found + [k ^ bit for k in found]
    return found


def exchange(value, axis, offset):
    size = lax.axis_size(axis)
    return lax.ppermute(value, axis, [(k, k ^ offset) for k in range(size)])


def per_device(field, forcing, slot_column, w_spec, skip_gain, bias):
    channels, planes, grid_len, _ = field.shape
    slabs, capacity = slot_column.shape
    groups = lax.axis_size("chan")
    own_rows = forcing.shape[1]
    factor = float(grid_len) ** -1.5

    row_np, col_np = plane_tables(grid_len)
    depth_np = depth_tables(planes, grid_len)
    rt = jnp.asarray(half_width(row_np))
    bd = jnp.asarray(half_width(np.swapaxes(row_np, 1, 2)) * ml_dtypes.bfloat16(factor))
    tx = jnp.asarray(half_width(col_np))
    txt = jnp.asarray(half_width(col_np.T))
    tz = jnp.asarray(half_width(depth_np))
    ts = jnp.asarray(half_width(np.swapaxes(depth_np, 1, 2)))
    table = jnp.asarray(half_width(spread_table()))
    table_t = jnp.asarray(half_width(spread_table().T))
    first = np.arange(slabs)[:, None] * planes * np.arange(KZ)[None, :] % grid_len
    first = np.repeat(first * (2.0 * math.pi / grid_len), KXY, axis=1)
    phases = jnp.asarray(np.stack([np.cos(first), np.sin(first)], 1).astype(np.float32))
    phase = lax.dynamic_index_in_dim(phases, lax.axis_index("slab"), 0, keepdims=False)

    slots = slot_column[:, None, :]
    me_slab, me_chan = lax.axis_index("slab"), lax.axis_index("chan")
    slab_bits = bits_of(slabs)
    routes = (slab_bits, slab_bits[-1:] + slab_bits[:-1])
    orders = [offsets(route) for route in routes]
    places = tuple(orders[1].index(offset) for offset in orders[0])
    gathered_slots = jnp.take(slots, me_slab ^ np.array(orders[0]), axis=0)

    forced_parts = [forcing]
    for bit in bits_of(groups):
        forced_parts += [exchange(part, "chan", bit) for part in forced_parts]
    forced_places = (me_chan ^ np.array(offsets(bits_of(groups)))).astype(jnp.int32)

    def send_sums(coefs, others):
        by_slot = to_slots(slots, coefs, others)
        return lax.all_to_all(by_slot, "slab", split_axis=0, concat_axis=0, tiled=True)

    def spread_spectra(own):
        pieces = [piece[None] for piece in jnp.split(own, 2, axis=0)]
        for step in range(len(slab_bits)):
            got = [exchange(piece, "slab", route[step]) for piece, route in zip(pieces, routes)]
            if step < len(slab_bits) - 1:
                pieces = [jnp.concatenate(pair, 0) for pair in zip(pieces, got)]
        return to_columns(gathered_slots, [pieces[0], got[0], pieces[1], got[1]], places, channels)

    tx_own = lax.dynamic_slice_in_dim(tx, lax.axis_index("chan") * own_rows, own_rows, 1)
    forced = analyse_forced(forcing, rt, tx_own, tz, phase, factor)
    others = [exchange(forced, "chan", k) for k in range(1, groups)]
    coefs = analyse(field, rt, tx, tz, phase, factor)
    sums = send_sums(coefs, [forced] + others)
    partial = mix(sums, w_spec, table, groups)
    for bit in reversed(bits_of(groups)):
        pairs = partial.reshape((partial.shape[0] // 2, 2) + partial.shape[1:])
        side = (me_chan // bit) % 2
        mine = lax.dynamic_index_in_dim(pairs, side, 1, keepdims=False)
        got = exchange(lax.dynamic_index_in_dim(pairs, 1 - side, 1, keepdims=False), "chan", bit)
        if mine.shape[0] > 1:
            partial = (mine.astype(F32) + got.astype(F32)).astype(BF16)
    spectra = spread_spectra(compress(mine[0], got[0], table_t))

    gain_rows = jnp.repeat(skip_gain, KXY)[:, None]
    centre = np.zeros((KXY, 2, ZB, KXY), np.float32)
    centre[KXY // 2, 0, :, KXY // 2] = 1.0 / factor
    centre = jnp.asarray(np.tile(centre.reshape(KXY, 2 * HALF), (channels, 1)))
    shift = centre * jnp.repeat(bias / skip_gain, KXY)[:, None]
    coefs_gelu = jnp.stack(
        [skip_gain**3 * (C1 * C2), skip_gain * C1, skip_gain * 0.5, skip_gain**2 * (6.0 * C1 * C2)], 1
    )
    output, grads, back = middle(
        spectra, field, forced_parts, forced_places, coefs_gelu, 1.0 / gain_rows, shift, rt, bd, tx, txt, tz, ts, phase, 0.5 * factor
    )
    doubling = jnp.where(jnp.arange(KZ) == 0, 1.0, 2.0).astype(F32)
    doubling = jnp.tile(jnp.repeat(doubling, channels), 2)[:, None]
    sums = jnp.sum(send_sums(back, []).astype(F32), axis=0)
    sums = (sums * doubling).astype(BF16)
    everyone = lax.all_gather(sums, "chan", axis=0)
    adjoint = spread_spectra(unmix(everyone, w_spec, table, table_t))
    gradient = finish(adjoint, grads, skip_gain * 0.5, bd, txt, ts, phase)
    return output, gradient


def solution(mesh):
    placed = (
        P("chan", "slab", None, None),
        P("slab", "chan", None),
        P(),
        P(None, "chan", None, "slab"),
        P("chan"),
        P("chan"),
    )
    return jax.shard_map(
        per_device,
        mesh=mesh,
        in_specs=placed,
        out_specs=(P("chan", "slab", None, None), P("chan", "slab", None, None)),
        check_vma=False,
    )
```

profile of v0, /device:TPU:0, one launch (start us, length us, event | category | flops | bytes accessed | tf_op | source)
XLA Modules:
  0.0 262.8 jit_solution(2537516630523557491)
XLA Ops:
  5.4 3.6 %forced.1.refs_0_ = bf16[32,1024]{1,0:T(8,128)(2,1)S(1)} custom-call(bf16[32,64,256]{2,1,0:T(8,128)(2,1)} %refs_2_.1, bf16[4,256,256]{2,1,0:T(8,128)(2,1)S(1)} %copy-done.3, bf16[64,64]{1,0:T(8,128)(2,1)S(1)} %constant_dynamic-slice_fusion.1.tx_ref, bf16[8,256,1024]{2,1,0:T(8,128)(2,1)S(1)} %copy-done, f32[2,512]{1,0:T(2,128)S(1)} %dynamic-slice_bitcast_fusion.2.ph_ref.refs_16_), custom_call_target="tpu_custom_call" | custom-call | tf_op jit(solution)/shard_map/forced/pallas_call | solution.py:213
  9.0 2.4 collective-permute-start.2
  12.2 17.0 %analyse.1.d_ref = bf16[256,1024]{1,0:T(8,128)(2,1)} custom-call(bf16[8,32,256,256]{3,2,1,0:T(8,128)(2,1)} %refs_1_.1, bf16[4,256,256]{2,1,0:T(8,128)(2,1)} %constant.125.clone.rt_ref.refs_10_, bf16[64,256]{1,0:T(8,128)(2,1)} %constant.127.clone.tx_ref.refs_12_, bf16[8,256,1024]{2,1,0:T(8,128)(2,1)} %constant.129.clone.tz_hbm.refs_14_, f32[2,512]{1,0:T(2,128)} %copy-done.10), custom_call_target="tpu_custom_call" | custom-call | flops 8589934592 | bytes 33554432 | tf_op jit(solution)/shard_map/analyse/pallas_call | solution.py:172
  30.3 3.7 %to_slots.2 = bf16[8,256,256]{2,1,0:T(8,128)(2,1)} custom-call(s32[8,1,256]{2,1,0:T(1,128)S(1)} %broadcast_in_dim.45.slots_ref, bf16[256,1024]{1,0:T(8,128)(2,1)S(1)} %copy-done.4, bf16[32,1024]{1,0:T(8,128)(2,1)S(1)} %forced.1.refs_0_, bf16[32,1024]{1,0:T(8,128)(2,1)S(1)} %collective-permute-done.refs_1_, ...), custom_call_target="tpu_custom_call" | custom-call | tf_op jit(solution)/shard_map/to_slots/pallas_call | solution.py:537
  34.0 6.1 %all-to-all-start = ((bf16[8,256,256]{2,1,0:T(8,128)(2,1)}), bf16[8,256,256]{2,1,0:T(8,128)(2,1)S(1)}, u32[]{:S(2)}, u32[]{:S(2)}) async-start(bf16[8,256,256]{2,1,0:T(8,128)(2,1)} %to_slots.2), calls=%async_computation | async-start | bytes 2097152 | tf_op jit(solution)/shard_map/all_to_all | solution.py:781
  41.6 24.7 %all-to-all-done.p_ref = bf16[8,256,256]{2,1,0:T(8,128)(2,1)S(1)} async-done(((bf16[8,256,256]{2,1,0:T(8,128)(2,1)}), bf16[8,256,256]{2,1,0:T(8,128)(2,1)S(1)}, u32[]{:S(2)}, u32[]{:S(2)}) %all-to-all-start) | async-done | bytes 1048608 | tf_op jit(solution)/shard_map/all_to_all | solution.py:781
  68.4 4.6 %mix.1 = bf16[4,2,8,4096]{3,2,1,0:T(8,128)(2,1)S(1)} custom-call(bf16[8,256,256]{2,1,0:T(8,128)(2,1)S(1)} %all-to-all-done.p_ref, bf16[2,8,32,4096]{3,2,1,0:T(8,128)(2,1)S(1)} %copy-done.1, bf16[128,2048]{1,0:T(8,128)(2,1)S(1)} %copy-done.6), custom_call_target="tpu_custom_call" | custom-call | flops 8388608 | bytes 4194304 | tf_op jit(solution)/shard_map/mix/pallas_call | solution.py:636
  76.4 4.0 %collective-permute-done.4 = bf16[1,2,8,4096]{3,2,1,0:T(8,128)(2,1)S(1)} collective-permute-done((bf16[1,2,8,4096]{3,2,1,0:T(8,128)(2,1)S(1)}, bf16[1,2,8,4096]{3,2,1,0:T(8,128)(2,1)S(1)}, u32[]{:S(2)}, u32[]{:S(2)}) %collective-permute-start.4) | collective-permute-done | bytes 131104 | tf_op jit(solution)/shard_map/ppermute | solution.py:741
  86.2 4.4 %collective-permute-done.5 = bf16[1,128,256]{2,1,0:T(8,128)(2,1)S(1)} collective-permute-done((bf16[1,128,256]{2,1,0:T(8,128)(2,1)S(1)}, bf16[1,128,256]{2,1,0:T(8,128)(2,1)S(1)}, u32[]{:S(2)}, u32[]{:S(2)}) %collective-permute-start.5) | collective-permute-done | bytes 65568 | tf_op jit(solution)/shard_map/ppermute | solution.py:741
  91.5 4.1 %collective-permute-done.6 = bf16[2,128,256]{2,1,0:T(8,128)(2,1)S(1)} collective-permute-done((bf16[2,128,256]{2,1,0:T(8,128)(2,1)S(1)}, bf16[2,128,256]{2,1,0:T(8,128)(2,1)S(1)}, u32[]{:S(2)}, u32[]{:S(2)}) %collective-permute-start.6) | collective-permute-done | bytes 131104 | tf_op jit(solution)/shard_map/ppermute | solution.py:741
  99.2 3.5 %collective-permute-done.7.refs_1_ = bf16[4,128,256]{2,1,0:T(8,128)(2,1)S(1)} collective-permute-done((bf16[4,128,256]{2,1,0:T(8,128)(2,1)S(1)}, bf16[4,128,256]{2,1,0:T(8,128)(2,1)S(1)}, u32[]{:S(2)}, u32[]{:S(2)}) %collective-permute-start.7) | collective-permute-done | bytes 262176 | tf_op jit(solution)/shard_map/ppermute | solution.py:741
  103.0 4.0 %to_columns.2.refs_0_ = bf16[256,1024]{1,0:T(8,128)(2,1)S(1)} custom-call(s32[8,1,256]{2,1,0:T(1,128)S(1)} %broadcast_select_fusion.slots_ref, bf16[4,128,256]{2,1,0:T(8,128)(2,1)S(1)} %pad_maximum_fusion.refs_0_, bf16[4,128,256]{2,1,0:T(8,128)(2,1)S(1)} %collective-permute-done.7.refs_1_, bf16[4,128,256]{2,1,0:T(8,128)(2,1)S(1)} %pad_maximum_fusion.1.refs_2_, ...), custom_call_target="tpu_custom_call" | custom-call | tf_op jit(solution)/shard_map/to_columns/pallas_call | solution.py:586
  107.8 52.3 %middle.1 = (bf16[8,32,256,256]{3,2,1,0:T(8,128)(2,1)}, bf16[8,32,256,256]{3,2,1,0:T(8,128)(2,1)}, bf16[256,1024]{1,0:T(8,128)(2,1)}) custom-call(bf16[256,1024]{1,0:T(8,128)(2,1)} %copy-done.8, bf16[8,32,256,256]{3,2,1,0:T(8,128)(2,1)} %refs_1_.1, bf16[32,64,256]{2,1,0:T(8,128)(2,1)} %refs_2_.1, bf16[32,64,256]{2,1,0:T(8,128)(2,1)} %collective-permute-done.11.refs_3_, ...), custom_call_target="tpu_custom_call" | custom-call | flops 17179869184 | bytes 33554432 | tf_op jit(solution)/shard_map/middle/pallas_call | solution.py:340
  161.2 3.7 %to_slots.3 = bf16[8,256,256]{2,1,0:T(8,128)(2,1)} custom-call(s32[8,1,256]{2,1,0:T(1,128)S(1)} %broadcast_in_dim.45.slots_ref, bf16[256,1024]{1,0:T(8,128)(2,1)S(1)} %copy-done.9), custom_call_target="tpu_custom_call" | custom-call | tf_op jit(solution)/shard_map/to_slots/pallas_call | solution.py:537
  164.9 5.7 %all-to-all-start.1 = ((bf16[8,256,256]{2,1,0:T(8,128)(2,1)}), bf16[8,256,256]{2,1,0:T(8,128)(2,1)S(1)}, u32[]{:S(2)}, u32[]{:S(2)}) async-start(bf16[8,256,256]{2,1,0:T(8,128)(2,1)} %to_slots.3), calls=%async_computation.1 | async-start | bytes 2097152 | tf_op jit(solution)/shard_map/all_to_all | solution.py:781
  170.7 21.6 %all-to-all-done.1 = bf16[8,256,256]{2,1,0:T(8,128)(2,1)S(1)} async-done(((bf16[8,256,256]{2,1,0:T(8,128)(2,1)}), bf16[8,256,256]{2,1,0:T(8,128)(2,1)S(1)}, u32[]{:S(2)}, u32[]{:S(2)}) %all-to-all-start.1) | async-done | bytes 1048608 | tf_op jit(solution)/shard_map/all_to_all | solution.py:781
  192.5 7.6 %all_gather.4.s_ref = bf16[4,256,256]{2,1,0:T(8,128)(2,1)S(1)} all-gather(bf16[1,256,256]{2,1,0:T(8,128)(2,1)S(1)} %fusion.1), channel_id=1, replica_groups=mesh['slab'=8,'chan'=4] {'chan'}, dimensions={0}, use_global_device_ids=true | all-gather | bytes 655360 | tf_op jit(solution)/shard_map/all_gather | solution.py:821
  202.3 7.1 %unmix.1 = bf16[256,256]{1,0:T(8,128)(2,1)S(1)} custom-call(bf16[4,256,256]{2,1,0:T(8,128)(2,1)S(1)} %all_gather.4.s_ref, bf16[2,8,32,4096]{3,2,1,0:T(8,128)(2,1)S(1)} %copy-done.2, bf16[128,2048]{1,0:T(8,128)(2,1)S(1)} %copy-done.6, bf16[2048,128]{1,0:T(8,128)(2,1)S(1)} %copy-done.7), custom_call_target="tpu_custom_call" | custom-call | flops 8388608 | bytes 4194304 | tf_op jit(solution)/shard_map/unmix/pallas_call | solution.py:711
  210.8 4.6 %collective-permute-done.14 = bf16[1,128,256]{2,1,0:T(8,128)(2,1)S(1)} collective-permute-done((bf16[1,128,256]{2,1,0:T(8,128)(2,1)S(1)}, bf16[1,128,256]{2,1,0:T(8,128)(2,1)S(1)}, u32[]{:S(2)}, u32[]{:S(2)}) %collective-permute-start.14) | collective-permute-done | bytes 65568 | tf_op jit(solution)/shard_map/ppermute | solution.py:741
  215.5 2.5 collective-permute-start.18
  218.0 4.9 %collective-permute-done.15 = bf16[2,128,256]{2,1,0:T(8,128)(2,1)S(1)} collective-permute-done((bf16[2,128,256]{2,1,0:T(8,128)(2,1)S(1)}, bf16[2,128,256]{2,1,0:T(8,128)(2,1)S(1)}, u32[]{:S(2)}, u32[]{:S(2)}) %collective-permute-start.15) | collective-permute-done | bytes 131104 | tf_op jit(solution)/shard_map/ppermute | solution.py:741
  224.9 5.6 %collective-permute-done.16.refs_1_ = bf16[4,128,256]{2,1,0:T(8,128)(2,1)S(1)} collective-permute-done((bf16[4,128,256]{2,1,0:T(8,128)(2,1)S(1)}, bf16[4,128,256]{2,1,0:T(8,128)(2,1)S(1)}, u32[]{:S(2)}, u32[]{:S(2)}) %collective-permute-start.16) | collective-permute-done | bytes 262176 | tf_op jit(solution)/shard_map/ppermute | solution.py:741
  231.2 4.0 %to_columns.3.q_ref = bf16[256,1024]{1,0:T(8,128)(2,1)S(1)} custom-call(s32[8,1,256]{2,1,0:T(1,128)S(1)} %broadcast_select_fusion.slots_ref, bf16[4,128,256]{2,1,0:T(8,128)(2,1)S(1)} %pad_maximum_fusion.2.refs_0_, bf16[4,128,256]{2,1,0:T(8,128)(2,1)S(1)} %collective-permute-done.16.refs_1_, bf16[4,128,256]{2,1,0:T(8,128)(2,1)S(1)} %pad_maximum_fusion.3.refs_2_, ...), custom_call_target="tpu_custom_call" | custom-call | tf_op jit(solution)/shard_map/to_columns/pallas_call | solution.py:586
  236.1 26.6 %finish.1 = bf16[8,32,256,256]{3,2,1,0:T(8,128)(2,1)} custom-call(bf16[256,1024]{1,0:T(8,128)(2,1)} %copy-done.5, bf16[8,32,256,256]{3,2,1,0:T(8,128)(2,1)} %get-tuple-element.7.g_ref, f32[8]{0:T(128)} %get-tuple-element.16.gain_ref, bf16[4,256,256]{2,1,0:T(8,128)(2,1)} %constant.126.clone.refs_11_.bd_ref, bf16[256,64]{1,0:T(8,128)(2,1)} %constant.128.clone.refs_13_.txt_ref, ...), custom_call_target="tpu_custom_call" | custom-call | flops 8589934592 | bytes 33554432 | tf_op jit(solution)/shard_map/finish/pallas_call | solution.py:425
  (104 shorter events, 33.4 us)
Async XLA Ops:
  0.6 90.0 %copy-start.16 = (s32[4]{0:T(128)S(1)}, s32[4]{0:T(128)}, u32[]{:S(2)}) copy-start(s32[4]{0:T(128)} %constant.135.clone) | copy-start | bytes 52
  5.4 92.9 %copy-start.12 = (f32[256,256]{1,0:T(8,128)S(1)}, f32[256,256]{1,0:T(8,128)}, u32[]{:S(2)}) copy-start(f32[256,256]{1,0:T(8,128)} %constant.136.clone) | copy-start | bytes 786436
  9.0 20.2 %collective-permute-start.2 = (bf16[32,1024]{1,0:T(8,128)(2,1)S(1)}, bf16[32,1024]{1,0:T(8,128)(2,1)S(1)}, u32[]{:S(2)}, u32[]{:S(2)}) collective-permute-start(bf16[32,1024]{1,0:T(8,128)(2,1)S(1)} %forced.1.refs_0_), channel_id=1, source_target_pairs={{0,3},{1,2},{2,1},{3,0},{4,7},{5,6},{6,5},{7,4},{8,11},{9,10},{10,... | collective-permute-start | bytes 196616 | tf_op jit(solution)/shard_map/ppermute | solution.py:741
  11.5 17.7 %collective-permute-start.1 = (bf16[32,1024]{1,0:T(8,128)(2,1)S(1)}, bf16[32,1024]{1,0:T(8,128)(2,1)S(1)}, u32[]{:S(2)}, u32[]{:S(2)}) collective-permute-start(bf16[32,1024]{1,0:T(8,128)(2,1)S(1)} %forced.1.refs_0_), channel_id=1, source_target_pairs={{0,2},{1,3},{2,0},{3,1},{4,6},{5,7},{6,4},{7,5},{8,10},{9,11},{10,... | collective-permute-start | bytes 196616 | tf_op jit(solution)/shard_map/ppermute | solution.py:741
  12.1 17.1 %collective-permute-start = (bf16[32,1024]{1,0:T(8,128)(2,1)S(1)}, bf16[32,1024]{1,0:T(8,128)(2,1)S(1)}, u32[]{:S(2)}, u32[]{:S(2)}) collective-permute-start(bf16[32,1024]{1,0:T(8,128)(2,1)S(1)} %forced.1.refs_0_), channel_id=1, source_target_pairs={{0,1},{1,0},{2,3},{3,2},{4,5},{5,4},{6,7},{7,6},{8,9},{9,8},{10,11... | collective-permute-start | bytes 196616 | tf_op jit(solution)/shard_map/ppermute | solution.py:741
  34.0 32.2 %all-to-all-start = ((bf16[8,256,256]{2,1,0:T(8,128)(2,1)}), bf16[8,256,256]{2,1,0:T(8,128)(2,1)S(1)}, u32[]{:S(2)}, u32[]{:S(2)}) async-start(bf16[8,256,256]{2,1,0:T(8,128)(2,1)} %to_slots.2), calls=%async_computation | async-start | bytes 2097152 | tf_op jit(solution)/shard_map/all_to_all | solution.py:781
  40.1 36.3 %collective-permute-start.11 = (bf16[32,64,256]{2,1,0:T(8,128)(2,1)}, bf16[32,64,256]{2,1,0:T(8,128)(2,1)}, u32[]{:S(2)}, u32[]{:S(2)}) collective-permute-start(bf16[32,64,256]{2,1,0:T(8,128)(2,1)} %refs_2_.1), channel_id=1, source_target_pairs={{0,2},{1,3},{2,0},{3,1},{4,6},{5,7},{6,4},{7,5},{8,10},{9,11},{10,... | collective-permute-start | bytes 3145736 | tf_op jit(solution)/shard_map/ppermute | solution.py:741
  41.6 66.2 %collective-permute-start.12 = (bf16[32,64,256]{2,1,0:T(8,128)(2,1)}, bf16[32,64,256]{2,1,0:T(8,128)(2,1)}, u32[]{:S(2)}, u32[]{:S(2)}) collective-permute-start(bf16[32,64,256]{2,1,0:T(8,128)(2,1)} %refs_2_.1), channel_id=1, source_target_pairs={{0,1},{1,0},{2,3},{3,2},{4,5},{5,4},{6,7},{7,6},{8,9},{9,8},{10,11... | collective-permute-start | bytes 3145736 | tf_op jit(solution)/shard_map/ppermute | solution.py:741
  73.1 1.6 collective-permute-start.3
  74.8 5.6 %collective-permute-start.4 = (bf16[1,2,8,4096]{3,2,1,0:T(8,128)(2,1)S(1)}, bf16[1,2,8,4096]{3,2,1,0:T(8,128)(2,1)S(1)}, u32[]{:S(2)}, u32[]{:S(2)}) collective-permute-start(bf16[1,2,8,4096]{3,2,1,0:T(8,128)(2,1)S(1)} %get-tuple-element.10), channel_id=1, source_target_pairs={{0,2},{1,3},{2,0},{3,1},{4,6},{5,7},{6,4},{7,5},{8,10},{9,11},{10,... | collective-permute-start | bytes 393224 | tf_op jit(solution)/shard_map/ppermute | solution.py:741
  76.4 31.5 %collective-permute-start.13 = (bf16[32,64,256]{2,1,0:T(8,128)(2,1)}, bf16[32,64,256]{2,1,0:T(8,128)(2,1)}, u32[]{:S(2)}, u32[]{:S(2)}) collective-permute-start(bf16[32,64,256]{2,1,0:T(8,128)(2,1)} %collective-permute-done.11.refs_3_), channel_id=1, source_target_pairs={{0,1},{1,0},{2,3},{3,2},{4,5},{5,4},{6,7},{7,6},{8,9},{9,8},{10,11... | collective-permute-start | bytes 3145736 | tf_op jit(solution)/shard_map/ppermute | solution.py:741
  81.2 4.3 %collective-permute-start.8 = (bf16[1,128,256]{2,1,0:T(8,128)(2,1)S(1)}, bf16[1,128,256]{2,1,0:T(8,128)(2,1)S(1)}, u32[]{:S(2)}, u32[]{:S(2)}) collective-permute-start(bf16[1,128,256]{2,1,0:T(8,128)(2,1)S(1)} %get-tuple-element.14), channel_id=1, source_target_pairs={{0,4},{4,0},{8,12},{12,8},{16,20},{20,16},{24,28},{28,24},{1,5},{5... | collective-permute-start | bytes 196616 | tf_op jit(solution)/shard_map/ppermute | solution.py:741
  83.1 7.4 %collective-permute-start.5 = (bf16[1,128,256]{2,1,0:T(8,128)(2,1)S(1)}, bf16[1,128,256]{2,1,0:T(8,128)(2,1)S(1)}, u32[]{:S(2)}, u32[]{:S(2)}) collective-permute-start(bf16[1,128,256]{2,1,0:T(8,128)(2,1)S(1)} %get-tuple-element.15), channel_id=1, source_target_pairs={{0,16},{4,20},{8,24},{12,28},{16,0},{20,4},{24,8},{28,12},{1,17},{... | collective-permute-start | bytes 196616 | tf_op jit(solution)/shard_map/ppermute | solution.py:741
  85.5 11.1 %collective-permute-start.9 = (bf16[2,128,256]{2,1,0:T(8,128)(2,1)S(1)}, bf16[2,128,256]{2,1,0:T(8,128)(2,1)S(1)}, u32[]{:S(2)}, u32[]{:S(2)}) collective-permute-start(bf16[2,128,256]{2,1,0:T(8,128)(2,1)S(1)} %pad_maximum_fusion.5), channel_id=1, source_target_pairs={{0,16},{4,20},{8,24},{12,28},{16,0},{20,4},{24,8},{28,12},{1,17},{... | collective-permute-start | bytes 393224 | tf_op jit(solution)/shard_map/ppermute | solution.py:741
  90.6 5.1 %collective-permute-start.6 = (bf16[2,128,256]{2,1,0:T(8,128)(2,1)S(1)}, bf16[2,128,256]{2,1,0:T(8,128)(2,1)S(1)}, u32[]{:S(2)}, u32[]{:S(2)}) collective-permute-start(bf16[2,128,256]{2,1,0:T(8,128)(2,1)S(1)} %pad_maximum_fusion.4), channel_id=1, source_target_pairs={{0,8},{4,12},{8,0},{12,4},{16,24},{20,28},{24,16},{28,20},{1,9},{5... | collective-permute-start | bytes 393224 | tf_op jit(solution)/shard_map/ppermute | solution.py:741
  95.7 7.0 %collective-permute-start.7 = (bf16[4,128,256]{2,1,0:T(8,128)(2,1)S(1)}, bf16[4,128,256]{2,1,0:T(8,128)(2,1)S(1)}, u32[]{:S(2)}, u32[]{:S(2)}) collective-permute-start(bf16[4,128,256]{2,1,0:T(8,128)(2,1)S(1)} %pad_maximum_fusion.refs_0_), channel_id=1, source_target_pairs={{0,4},{4,0},{8,12},{12,8},{16,20},{20,16},{24,28},{28,24},{1,5},{5... | collective-permute-start | bytes 786440 | tf_op jit(solution)/shard_map/ppermute | solution.py:741
  96.6 6.4 %collective-permute-start.10 = (bf16[4,128,256]{2,1,0:T(8,128)(2,1)S(1)}, bf16[4,128,256]{2,1,0:T(8,128)(2,1)S(1)}, u32[]{:S(2)}, u32[]{:S(2)}) collective-permute-start(bf16[4,128,256]{2,1,0:T(8,128)(2,1)S(1)} %pad_maximum_fusion.1.refs_2_), channel_id=1, source_target_pairs={{0,8},{4,12},{8,0},{12,4},{16,24},{20,28},{24,16},{28,20},{1,9},{5... | collective-permute-start | bytes 786440 | tf_op jit(solution)/shard_map/ppermute | solution.py:741
  164.9 27.4 %all-to-all-start.1 = ((bf16[8,256,256]{2,1,0:T(8,128)(2,1)}), bf16[8,256,256]{2,1,0:T(8,128)(2,1)S(1)}, u32[]{:S(2)}, u32[]{:S(2)}) async-start(bf16[8,256,256]{2,1,0:T(8,128)(2,1)} %to_slots.3), calls=%async_computation.1 | async-start | bytes 2097152 | tf_op jit(solution)/shard_map/all_to_all | solution.py:781
  209.4 6.0 %collective-permute-start.14 = (bf16[1,128,256]{2,1,0:T(8,128)(2,1)S(1)}, bf16[1,128,256]{2,1,0:T(8,128)(2,1)S(1)}, u32[]{:S(2)}, u32[]{:S(2)}) collective-permute-start(bf16[1,128,256]{2,1,0:T(8,128)(2,1)S(1)} %get-tuple-element.13), channel_id=1, source_target_pairs={{0,16},{4,20},{8,24},{12,28},{16,0},{20,4},{24,8},{28,12},{1,17},{... | collective-permute-start | bytes 196616 | tf_op jit(solution)/shard_map/ppermute | solution.py:741
  209.5 6.0 %collective-permute-start.17 = (bf16[1,128,256]{2,1,0:T(8,128)(2,1)S(1)}, bf16[1,128,256]{2,1,0:T(8,128)(2,1)S(1)}, u32[]{:S(2)}, u32[]{:S(2)}) collective-permute-start(bf16[1,128,256]{2,1,0:T(8,128)(2,1)S(1)} %get-tuple-element.12), channel_id=1, source_target_pairs={{0,4},{4,0},{8,12},{12,8},{16,20},{20,16},{24,28},{28,24},{1,5},{5... | collective-permute-start | bytes 196616 | tf_op jit(solution)/shard_map/ppermute | solution.py:741
  215.4 7.6 %collective-permute-start.15 = (bf16[2,128,256]{2,1,0:T(8,128)(2,1)S(1)}, bf16[2,128,256]{2,1,0:T(8,128)(2,1)S(1)}, u32[]{:S(2)}, u32[]{:S(2)}) collective-permute-start(bf16[2,128,256]{2,1,0:T(8,128)(2,1)S(1)} %pad_maximum_fusion.6), channel_id=1, source_target_pairs={{0,8},{4,12},{8,0},{12,4},{16,24},{20,28},{24,16},{28,20},{1,9},{5... | collective-permute-start | bytes 393224 | tf_op jit(solution)/shard_map/ppermute | solution.py:741
  215.5 9.3 %collective-permute-start.18 = (bf16[2,128,256]{2,1,0:T(8,128)(2,1)S(1)}, bf16[2,128,256]{2,1,0:T(8,128)(2,1)S(1)}, u32[]{:S(2)}, u32[]{:S(2)}) collective-permute-start(bf16[2,128,256]{2,1,0:T(8,128)(2,1)S(1)} %pad_maximum_fusion.7), channel_id=1, source_target_pairs={{0,16},{4,20},{8,24},{12,28},{16,0},{20,4},{24,8},{28,12},{1,17},{... | collective-permute-start | bytes 393224 | tf_op jit(solution)/shard_map/ppermute | solution.py:741
  223.0 7.5 %collective-permute-start.16 = (bf16[4,128,256]{2,1,0:T(8,128)(2,1)S(1)}, bf16[4,128,256]{2,1,0:T(8,128)(2,1)S(1)}, u32[]{:S(2)}, u32[]{:S(2)}) collective-permute-start(bf16[4,128,256]{2,1,0:T(8,128)(2,1)S(1)} %pad_maximum_fusion.2.refs_0_), channel_id=1, source_target_pairs={{0,4},{4,0},{8,12},{12,8},{16,20},{20,16},{24,28},{28,24},{1,5},{5... | collective-permute-start | bytes 786440 | tf_op jit(solution)/shard_map/ppermute | solution.py:741
  224.8 6.4 %collective-permute-start.19 = (bf16[4,128,256]{2,1,0:T(8,128)(2,1)S(1)}, bf16[4,128,256]{2,1,0:T(8,128)(2,1)S(1)}, u32[]{:S(2)}, u32[]{:S(2)}) collective-permute-start(bf16[4,128,256]{2,1,0:T(8,128)(2,1)S(1)} %pad_maximum_fusion.3.refs_2_), channel_id=1, source_target_pairs={{0,8},{4,12},{8,0},{12,4},{16,24},{20,28},{24,16},{28,20},{1,9},{5... | collective-permute-start | bytes 786440 | tf_op jit(solution)/shard_map/ppermute | solution.py:741
  (15 other events, 422.9 us)
where the time goes:
time: 264 us; the launch traced here: 263 us
  Pallas kernels  127 us (48%)
  waiting for transfers between devices  82.4 us (31%)
  starting transfers between devices  26.2 us (10%)
  local copies, waits for them, and re-layouts  15 us (6%)
  blocking collectives  7.61 us (3%)
  other arithmetic  3.13 us (1%)
    pallas_call x1, Pallas kernels, middle(): pl.pallas_call(functools.partial(middle_kernel, factor, parts), in_specs=...  52.3 us
    all_to_all x2, waiting for transfers between devices, send_sums(): lax.all_to_all(by_slot, 'slab', split_axis=0, concat_axis=0, tiled=True)  46.2 us
    ppermute x20, waiting for transfers between devices, exchange(): return lax.ppermute(value, axis, [(k, k ^ offset) for k in range(size)])  36.2 us
    pallas_call x1, Pallas kernels, finish(): pl.pallas_call(finish_kernel, in_specs=[resident(), anywhere(), scalars()...  26.6 us
    pallas_call x1, Pallas kernels, analyse(): pl.pallas_call(functools.partial(analyse_kernel, factor), in_specs=[anywh...  17 us
    ppermute x20, starting transfers between devices, exchange(): return lax.ppermute(value, axis, [(k, k ^ offset) for k in range(size)])  14.5 us
    all_to_all x2, starting transfers between devices, send_sums(): lax.all_to_all(by_slot, 'slab', split_axis=0, concat_axis=0, tiled=True)  11.7 us
    unnamed x34, local copies, waits for them, and re-layouts  11.3 us
  transfers between devices with their start and end apart: 22, of which 14 were waited for; matrix products, arithmetic and copies ran while one was open for 2% of the time, Pallas kernels for 10%

commit v1 on v0

--- a/solution.py
+++ b/solution.py
@@ -21,6 +21,7 @@
 SLOTS = 128
 SMALL = 16 * 2**20
 LARGE = 54 * 2**20
+AHEAD = 2
 
 
 def dot(a, b):
@@ -185,7 +186,7 @@
         ],
         compiler_params=pltpu.CompilerParams(vmem_limit_bytes=LARGE),
         cost_estimate=pl.CostEstimate(
-            flops=512 * volume.size, bytes_accessed=2 * volume.size, transcendentals=0
+            flops=8 * volume.size, bytes_accessed=volume.size // 8, transcendentals=0
         ),
         name="analyse",
     )(volume, rt, tx, tz, phase)
@@ -240,6 +241,13 @@
 def send_block(buf_ref, o_ref, sems, b):
     slot = lax.rem(b, 2)
     return pltpu.make_async_copy(buf_ref.at[slot], o_ref.at[:, pl.ds(b * ZB, ZB)], sems.at[slot])
+
+
+def send_half(buf_ref, o_ref, sems, b, h):
+    slot = lax.rem(b, 2)
+    half = buf_ref.shape[1] // 2
+    part = pl.ds(h * half, half)
+    return pltpu.make_async_copy(buf_ref.at[slot, part], o_ref.at[part, pl.ds(b * ZB, ZB)], sems.at[slot, h])
 
 
 def fetch_forced(f_refs, raw_ref, sems, b, slot):
@@ -402,21 +410,25 @@
 
         @pl.when(b > 1)
         def _():
-            send_block(buf_ref, o_ref, sems, b - 2).wait()
+            for h in range(2):
+                send_half(buf_ref, o_ref, sems, b - 2, h).wait()
 
         zz_ref[...] = dot(turned_ref[...], ts_ref[slot]).astype(BF16)
         for c in range(channels):
             x_ref[c] = column_fields(zz_ref, txt, c)
         for c in range(channels):
+            if c == channels // 2:
+                send_half(buf_ref, o_ref, sems, b, 0).start()
             for i in range(ZB):
                 plane = kept_ref[slot, c, i].astype(F32)
                 buf_ref[lax.rem(b, 2), c, i] = (dot(x_ref[c], bd_ref[i]) + gain_ref[c] * plane).astype(BF16)
-        send_block(buf_ref, o_ref, sems, b).start()
+        send_half(buf_ref, o_ref, sems, b, 1).start()
         return carry
 
     lax.fori_loop(0, blocks, body, 0)
     for b in (blocks - 2, blocks - 1):
-        send_block(buf_ref, o_ref, sems, b).wait()
+        for h in range(2):
+            send_half(buf_ref, o_ref, sems, b, h).wait()
 
 
 def finish(spectra, grads, gain, bd, txt, ts, phase):
@@ -434,7 +446,7 @@
             pltpu.VMEM((3, channels, ZB, rows, grid_len), BF16),
             pltpu.VMEM((2, channels, ZB, rows, grid_len), BF16),
             pltpu.VMEM((3,) + ts.shape[1:], BF16),
-            pltpu.SemaphoreType.DMA((2,)),
+            pltpu.SemaphoreType.DMA((2, 2)),
             pltpu.SemaphoreType.DMA((3,)),
             pltpu.SemaphoreType.DMA((3,)),
         ],
@@ -499,8 +511,8 @@
     return (iota(shape, 0) == iota(shape, 2) // KXY).astype(F32)
 
 
-def to_slots_kernel(slots_ref, d_ref, *refs):
-    others, (o_ref, t_ref) = refs[:-2], refs[-2:]
+def to_slots_kernel(places, unread, slots_ref, d_ref, *refs):
+    others, a_refs, b_refs, t_ref = refs[: -5 - unread], refs[-5:-3], refs[-3:-1], refs[-1]
     channels = d_ref.shape[0] // KXY
     data = d_ref[...]
     if others:
@@ -528,19 +540,23 @@
         row, lane = iota(shape, 0), iota(shape, 1)
         keep = (row // channels == lane // GROUP) & (row % channels == lane % GROUP)
         table = dot(one_hot(keep), table).astype(BF16)
-    for k in range(slots_ref.shape[0]):
-        o_ref[k] = dot(table, chosen(slots_ref, k, KXY * KXY)).astype(BF16)
-
-
-def to_slots(slots, coefs, others):
+    half, rows = len(places) // 2, table.shape[0] // 2
+    for k, place in enumerate(places):
+        out = dot(table, chosen(slots_ref, k, KXY * KXY)).astype(BF16)
+        a_refs[k // half][k % half] = out[:rows]
+        b_refs[place // half][place % half] = out[rows:]
+
+
+def to_slots(slots, coefs, others, places, after):
     slabs, _, capacity = slots.shape
     return pl.pallas_call(
-        to_slots_kernel,
-        out_shape=jax.ShapeDtypeStruct((slabs, coefs.shape[0], capacity), BF16),
+        functools.partial(to_slots_kernel, places, len(after)),
+        in_specs=[resident()] * (2 + len(others)) + [anywhere()] * len(after),
+        out_shape=[jax.ShapeDtypeStruct((slabs // 2, coefs.shape[0] // 2, capacity), BF16)] * 4,
         scratch_shapes=[pltpu.VMEM((WIDE, KXY * KXY), F32)],
         compiler_params=pltpu.CompilerParams(vmem_limit_bytes=SMALL),
         name="to_slots",
-    )(slots, coefs, *others)
+    )(slots, coefs, *others, *after)
 
 
 def to_columns_kernel(places, slots_ref, *refs):
@@ -597,23 +613,32 @@
     return pltpu.make_async_copy(hbm_ref.at[:, :, :, lanes], w_ref.at[:, :, :, lanes], sems.at[k])
 
 
-def mix_kernel(groups, p_ref, w_hbm, e_ref, o_ref, s_ref, w_ref, sems):
+def fetch_ahead(w_hbm, w_ref, sems, k):
+    chunks = w_ref.shape[-1] // LANES
+
+    @pl.when(k + AHEAD < chunks)
+    def _():
+        fetch_lanes(w_hbm, w_ref, sems, k + AHEAD).start()
+
+    fetch_lanes(w_hbm, w_ref, sems, k).wait()
+
+
+def mix_kernel(groups, a_ref, b_ref, c_ref, d_ref, w_hbm, e_ref, o_ref, s_ref, w_ref, sems):
     channels, outs, length = w_ref.shape[1:]
-    for k in range(length // LANES):
+    for k in range(min(AHEAD, length // LANES)):
         fetch_lanes(w_hbm, w_ref, sems, k).start()
     own = outs // groups
     mask = depth_mask(LANES)
     per = SLOTS * KZ // LANES
-    total = p_ref[0].astype(F32)
-    for k in range(1, p_ref.shape[0]):
-        total += p_ref[k].astype(F32)
-    s_ref[...] = total.astype(BF16)
+    rows = a_ref.shape[1]
+    s_ref[:rows] = (a_ref[0].astype(F32) + b_ref[0].astype(F32)).astype(BF16)
+    s_ref[rows:] = (c_ref[0].astype(F32) + d_ref[0].astype(F32)).astype(BF16)
 
     def body(k, carry):
         slot = pl.multiple_of(k // per * SLOTS, SLOTS)
         part = pl.multiple_of(k % per * LANES, LANES)
         lane = pl.multiple_of(k * LANES, LANES)
-        fetch_lanes(w_hbm, w_ref, sems, k).wait()
+        fetch_ahead(w_hbm, w_ref, sems, k)
         u = spread(s_ref[:, pl.ds(slot, SLOTS)], e_ref[:, pl.ds(part, LANES)], mask, channels)
         real = jnp.zeros((outs, LANES), F32)
         imag = jnp.zeros((outs, LANES), F32)
@@ -636,9 +661,9 @@
     return pl.pallas_call(
         functools.partial(mix_kernel, groups),
         out_shape=jax.ShapeDtypeStruct((groups, 2, outs // groups, length), BF16),
-        in_specs=[resident(), anywhere(), resident()],
+        in_specs=[resident()] * 4 + [anywhere(), resident()],
         scratch_shapes=[
-            pltpu.VMEM(sums.shape[1:], BF16),
+            pltpu.VMEM((2 * sums[0].shape[1], sums[0].shape[2]), BF16),
             pltpu.VMEM(weights.shape, BF16),
             pltpu.SemaphoreType.DMA((length // LANES,)),
         ],
@@ -647,7 +672,7 @@
             flops=4 * weights.size, bytes_accessed=2 * weights.size, transcendentals=0
         ),
         name="mix",
-    )(sums, weights, table)
+    )(*sums, weights, table)
 
 
 def compress_kernel(a_ref, b_ref, et_ref, o_ref):
@@ -674,7 +699,7 @@
 
 def unmix_kernel(s_ref, w_hbm, e_ref, et_ref, o_ref, adj_ref, w_ref, sems):
     channels, outs, length = w_ref.shape[1:]
-    for k in range(length // LANES):
+    for k in range(min(AHEAD, length // LANES)):
         fetch_lanes(w_hbm, w_ref, sems, k).start()
     groups = s_ref.shape[0]
     mask = depth_mask(LANES)
@@ -686,7 +711,7 @@
             slot = pl.multiple_of(k * SLOTS, SLOTS)
             part = pl.multiple_of(j * LANES, LANES)
             lane = pl.multiple_of(k * SLOTS * KZ + j * LANES, LANES)
-            fetch_lanes(w_hbm, w_ref, sems, k * per + j).wait()
+            fetch_ahead(w_hbm, w_ref, sems, k * per + j)
             table = e_ref[:, pl.ds(part, LANES)]
             pieces = [spread(s_ref[g, :, pl.ds(slot, SLOTS)], table, mask, outs // groups) for g in range(groups)]
             gr = jnp.concatenate([piece[0] for piece in pieces], 0)
@@ -776,9 +801,15 @@
         forced_parts += [exchange(part, "chan", bit) for part in forced_parts]
     forced_places = (me_chan ^ np.array(offsets(bits_of(groups)))).astype(jnp.int32)
 
-    def send_sums(coefs, others):
-        by_slot = to_slots(slots, coefs, others)
-        return lax.all_to_all(by_slot, "slab", split_axis=0, concat_axis=0, tiled=True)
+    def send_sums(coefs, others, after):
+        parts = to_slots(gathered_slots, coefs, others, places, after)
+        kept, sent = [parts[0], parts[2]], [parts[1], parts[3]]
+        for step in reversed(range(len(slab_bits))):
+            got = [exchange(part, "slab", route[step]) for part, route in zip(sent, routes)]
+            if step == 0:
+                return kept[0], got[0], kept[1], got[1]
+            sums = [(mine.astype(F32) + other.astype(F32)).astype(BF16) for mine, other in zip(kept, got)]
+            kept, sent = zip(*[jnp.split(part, 2, axis=0) for part in sums])
 
     def spread_spectra(own):
         pieces = [piece[None] for piece in jnp.split(own, 2, axis=0)]
@@ -792,8 +823,7 @@
     forced = analyse_forced(forcing, rt, tx_own, tz, phase, factor)
     others = [exchange(forced, "chan", k) for k in range(1, groups)]
     coefs = analyse(field, rt, tx, tz, phase, factor)
-    sums = send_sums(coefs, [forced] + others)
-    partial = mix(sums, w_spec, table, groups)
+    partial = mix(send_sums(coefs, [forced] + others, forced_parts[1:2]), w_spec, table, groups)
     for bit in reversed(bits_of(groups)):
         pairs = partial.reshape((partial.shape[0] // 2, 2) + partial.shape[1:])
         side = (me_chan // bit) % 2
@@ -816,7 +846,8 @@
     )
     doubling = jnp.where(jnp.arange(KZ) == 0, 1.0, 2.0).astype(F32)
     doubling = jnp.tile(jnp.repeat(doubling, channels), 2)[:, None]
-    sums = jnp.sum(send_sums(back, []).astype(F32), axis=0)
+    parts = [part[0].astype(F32) for part in send_sums(back, [], [])]
+    sums = jnp.concatenate([parts[0] + parts[1], parts[2] + parts[3]], 0)
     sums = (sums * doubling).astype(BF16)
     everyone = lax.all_gather(sums, "chan", axis=0)
     adjoint = spread_spectra(unmix(everyone, w_spec, table, table_t))

time: 264 us -> 251 us (0.951)
  waiting for transfers between devices: 82.4 us -> 64.5 us
  starting transfers between devices: 26.2 us -> 30.7 us
  local copies, waits for them, and re-layouts: 15 us -> 18.7 us
  Pallas kernels: 127 us -> 124 us
    all_to_all x2 -> x0, waiting for transfers between devices: 46.2 us -> none  [send_sums(): lax.all_to_all(by_slot, 'slab', split_axis=0, concat_axis=0, tiled=True)]
    ppermute x20 -> x32, waiting for transfers between devices: 36.2 us -> 64.5 us  [exchange(): return lax.ppermute(value, axis, [(k, k ^ offset) for k in range(size)])]
    ppermute x20 -> x32, starting transfers between devices: 14.5 us -> 30.7 us  [exchange(): return lax.ppermute(value, axis, [(k, k ^ offset) for k in range(size)])]
    all_to_all x2 -> x0, starting transfers between devices: 11.7 us -> none  [send_sums(): lax.all_to_all(by_slot, 'slab', split_axis=0, concat_axis=0, tiled=True)]
    unnamed x34 -> x38, local copies, waits for them, and re-layouts: 11.3 us -> 12.5 us
  transfers between devices with their start and end apart: 22 -> 32, of which waited for: 14 -> 22; matrix products, arithmetic and copies ran while one was open for 2% -> 4% of each run, Pallas kernels for 10% -> 10%
where the time goes in v1:
time: 251 us; the launch traced here: 250 us
  Pallas kernels  124 us (49%)
  waiting for transfers between devices  64.5 us (26%)
  starting transfers between devices  30.7 us (12%)
  local copies, waits for them, and re-layouts  18.7 us (7%)
  blocking collectives  6.51 us (3%)
  other arithmetic  4.75 us (2%)
    ppermute x32, waiting for transfers between devices, exchange(): return lax.ppermute(value, axis, [(k, k ^ offset) for k in range(size)])  64.5 us
    pallas_call x1, Pallas kernels, middle(): pl.pallas_call(functools.partial(middle_kernel, factor, parts), in_specs=...  52.3 us
    ppermute x32, starting transfers between devices, exchange(): return lax.ppermute(value, axis, [(k, k ^ offset) for k in range(size)])  30.7 us
    pallas_call x1, Pallas kernels, finish(): pl.pallas_call(finish_kernel, in_specs=[resident(), anywhere(), scalars()...  26.2 us
    pallas_call x1, Pallas kernels, analyse(): pl.pallas_call(functools.partial(analyse_kernel, factor), in_specs=[anywh...  17 us
    unnamed x38, local copies, waits for them, and re-layouts  12.5 us
    pallas_call x2, Pallas kernels, to_columns(): pl.pallas_call(functools.partial(to_columns_kernel, places), out_shape=ja...  7.96 us
    pallas_call x1, Pallas kernels, unmix(): pl.pallas_call(unmix_kernel, out_shape=jax.ShapeDtypeStruct((2 * KZ * cha...  7.12 us
  transfers between devices with their start and end apart: 32, of which 22 were waited for; matrix products, arithmetic and copies ran while one was open for 4% of the time, Pallas kernels for 10%

profile of v1, /device:TPU:0, one launch (start us, length us, event | category | flops | bytes accessed | tf_op | source)
XLA Modules:
  0.0 250.4 jit_solution(9445066909209251663)
XLA Ops:
  0.7 3.0 %collective-permute-start.3 = (bf16[32,64,256]{2,1,0:T(8,128)(2,1)}, bf16[32,64,256]{2,1,0:T(8,128)(2,1)}, u32[]{:S(2)}, u32[]{:S(2)}) collective-permute-start(bf16[32,64,256]{2,1,0:T(8,128)(2,1)} %refs_2_.1), channel_id=1, source_target_pairs={{0,2},{1,3},{2,0},{3,1},{4,6},{5,7},{6,4},{7,5},{8,10},{9,11},{10,... | collective-permute-start | bytes 3145736 | tf_op jit(solution)/shard_map/ppermute | solution.py:766
  15.2 17.0 %analyse.1.d_ref = bf16[256,1024]{1,0:T(8,128)(2,1)} custom-call(bf16[8,32,256,256]{3,2,1,0:T(8,128)(2,1)} %refs_1_.1, bf16[4,256,256]{2,1,0:T(8,128)(2,1)} %constant.123.clone.rt_ref.refs_10_, bf16[64,256]{1,0:T(8,128)(2,1)} %constant.125.clone.tx_ref.refs_12_, bf16[8,256,1024]{2,1,0:T(8,128)(2,1)} %constant.127.clone.tz_hbm.refs_14_, f32[2,512]{1,0:T(2,128)} %copy-done.14), custom_call_target="tpu_custom_call" | custom-call | flops 134217728 | bytes 2097152 | tf_op jit(solution)/shard_map/analyse/pallas_call | solution.py:173
  33.3 2.8 %to_slots.2 = (bf16[4,128,256]{2,1,0:T(8,128)(2,1)S(1)}, bf16[4,128,256]{2,1,0:T(8,128)(2,1)S(1)}, bf16[4,128,256]{2,1,0:T(8,128)(2,1)S(1)}, bf16[4,128,256]{2,1,0:T(8,128)(2,1)S(1)}) custom-call(s32[8,1,256]{2,1,0:T(1,128)S(1)} %broadcast_select_fusion.slots_ref, bf16[256,1024]{1,0:T(8,128)(2,1)S(1)} %copy-done.6, bf16[32,1024]{1,0:T(8,128)(2,1)S(1)} %forced.1.refs_0_, ...), custom_call_target="tpu_custom_call" | custom-call | tf_op jit(solution)/shard_map/to_slots/pallas_call | solution.py:552
  39.2 5.1 %collective-permute-done.4 = bf16[4,128,256]{2,1,0:T(8,128)(2,1)S(1)} collective-permute-done((bf16[4,128,256]{2,1,0:T(8,128)(2,1)S(1)}, bf16[4,128,256]{2,1,0:T(8,128)(2,1)S(1)}, u32[]{:S(2)}, u32[]{:S(2)}) %collective-permute-start.4) | collective-permute-done | bytes 262176 | tf_op jit(solution)/shard_map/ppermute | solution.py:766
  46.2 2.7 %collective-permute-start.8 = (bf16[2,128,256]{2,1,0:T(8,128)(2,1)S(1)}, bf16[2,128,256]{2,1,0:T(8,128)(2,1)S(1)}, u32[]{:S(2)}, u32[]{:S(2)}) collective-permute-start(bf16[2,128,256]{2,1,0:T(8,128)(2,1)S(1)} %split.85), channel_id=1, source_target_pairs={{0,16},{4,20},{8,24},{12,28},{16,0},{20,4},{24,8},{28,12},{1,17},{... | collective-permute-start | bytes 393224 | tf_op jit(solution)/shard_map/ppermute | solution.py:766
  57.3 2.7 %collective-permute-done.9.d_ref = bf16[1,128,256]{2,1,0:T(8,128)(2,1)S(1)} collective-permute-done((bf16[1,128,256]{2,1,0:T(8,128)(2,1)S(1)}, bf16[1,128,256]{2,1,0:T(8,128)(2,1)S(1)}, u32[]{:S(2)}, u32[]{:S(2)}) %collective-permute-start.9) | collective-permute-done | bytes 65568 | tf_op jit(solution)/shard_map/ppermute | solution.py:766
  62.2 4.7 %mix.1 = bf16[4,2,8,4096]{3,2,1,0:T(8,128)(2,1)S(1)} custom-call(bf16[1,128,256]{2,1,0:T(8,128)(2,1)S(1)} %get-tuple-element.35.a_ref, bf16[1,128,256]{2,1,0:T(8,128)(2,1)S(1)} %collective-permute-done.6.b_ref, bf16[1,128,256]{2,1,0:T(8,128)(2,1)S(1)} %get-tuple-element.33.c_ref, bf16[1,128,256]{2,1,0:T(8,128)(2,1)S(1)} %collective-permute-done.9.d_ref, ...), custom_call_target="tpu_custom_call" | custom-call | flops 8388608 | bytes 4194304 | tf_op jit(solution)/shard_map/mix/pallas_call | solution.py:661
  71.0 3.3 %collective-permute-done.11 = bf16[1,2,8,4096]{3,2,1,0:T(8,128)(2,1)S(1)} collective-permute-done((bf16[1,2,8,4096]{3,2,1,0:T(8,128)(2,1)S(1)}, bf16[1,2,8,4096]{3,2,1,0:T(8,128)(2,1)S(1)}, u32[]{:S(2)}, u32[]{:S(2)}) %collective-permute-start.11) | collective-permute-done | bytes 131104 | tf_op jit(solution)/shard_map/ppermute | solution.py:766
  80.3 6.1 %collective-permute-done.12 = bf16[1,128,256]{2,1,0:T(8,128)(2,1)S(1)} collective-permute-done((bf16[1,128,256]{2,1,0:T(8,128)(2,1)S(1)}, bf16[1,128,256]{2,1,0:T(8,128)(2,1)S(1)}, u32[]{:S(2)}, u32[]{:S(2)}) %collective-permute-start.12) | collective-permute-done | bytes 65568 | tf_op jit(solution)/shard_map/ppermute | solution.py:766
  88.4 4.4 %collective-permute-done.13 = bf16[2,128,256]{2,1,0:T(8,128)(2,1)S(1)} collective-permute-done((bf16[2,128,256]{2,1,0:T(8,128)(2,1)S(1)}, bf16[2,128,256]{2,1,0:T(8,128)(2,1)S(1)}, u32[]{:S(2)}, u32[]{:S(2)}) %collective-permute-start.13) | collective-permute-done | bytes 131104 | tf_op jit(solution)/shard_map/ppermute | solution.py:766
  99.4 4.0 %to_columns.2.refs_0_ = bf16[256,1024]{1,0:T(8,128)(2,1)S(1)} custom-call(s32[8,1,256]{2,1,0:T(1,128)S(1)} %broadcast_select_fusion.slots_ref, bf16[4,128,256]{2,1,0:T(8,128)(2,1)S(1)} %pad_maximum_fusion.refs_0_, bf16[4,128,256]{2,1,0:T(8,128)(2,1)S(1)} %collective-permute-done.14.refs_1_, bf16[4,128,256]{2,1,0:T(8,128)(2,1)S(1)} %pad_maximum_fusion.1.refs_2_, ...), custom_call_target="tpu_custom_call" | custom-call | tf_op jit(solution)/shard_map/to_columns/pallas_call | solution.py:602
  104.2 52.3 %middle.1 = (bf16[8,32,256,256]{3,2,1,0:T(8,128)(2,1)}, bf16[8,32,256,256]{3,2,1,0:T(8,128)(2,1)}, bf16[256,1024]{1,0:T(8,128)(2,1)}) custom-call(bf16[256,1024]{1,0:T(8,128)(2,1)} %copy-done.12, bf16[8,32,256,256]{3,2,1,0:T(8,128)(2,1)} %refs_1_.1, bf16[32,64,256]{2,1,0:T(8,128)(2,1)} %refs_2_.1, ...), custom_call_target="tpu_custom_call" | custom-call | flops 17179869184 | bytes 33554432 | tf_op jit(solution)/shard_map/middle/pallas_call | solution.py:348
  157.6 2.7 %to_slots.3 = (bf16[4,128,256]{2,1,0:T(8,128)(2,1)S(1)}, bf16[4,128,256]{2,1,0:T(8,128)(2,1)S(1)}, bf16[4,128,256]{2,1,0:T(8,128)(2,1)S(1)}, bf16[4,128,256]{2,1,0:T(8,128)(2,1)S(1)}) custom-call(s32[8,1,256]{2,1,0:T(1,128)S(1)} %broadcast_select_fusion.slots_ref, bf16[256,1024]{1,0:T(8,128)(2,1)S(1)} %copy-done.13), custom_call_target="tpu_custom_call" | custom-call | tf_op jit(solution)/shard_map/to_slots/pallas_call | solution.py:552
  162.7 4.0 %collective-permute-done.20 = bf16[4,128,256]{2,1,0:T(8,128)(2,1)S(1)} collective-permute-done((bf16[4,128,256]{2,1,0:T(8,128)(2,1)S(1)}, bf16[4,128,256]{2,1,0:T(8,128)(2,1)S(1)}, u32[]{:S(2)}, u32[]{:S(2)}) %collective-permute-start.20) | collective-permute-done | bytes 262176 | tf_op jit(solution)/shard_map/ppermute | solution.py:766
  167.0 3.4 %collective-permute-done.23 = bf16[4,128,256]{2,1,0:T(8,128)(2,1)S(1)} collective-permute-done((bf16[4,128,256]{2,1,0:T(8,128)(2,1)S(1)}, bf16[4,128,256]{2,1,0:T(8,128)(2,1)S(1)}, u32[]{:S(2)}, u32[]{:S(2)}) %collective-permute-start.23) | collective-permute-done | bytes 262176 | tf_op jit(solution)/shard_map/ppermute | solution.py:766
  173.5 3.2 %collective-permute-done.24 = bf16[2,128,256]{2,1,0:T(8,128)(2,1)S(1)} collective-permute-done((bf16[2,128,256]{2,1,0:T(8,128)(2,1)S(1)}, bf16[2,128,256]{2,1,0:T(8,128)(2,1)S(1)}, u32[]{:S(2)}, u32[]{:S(2)}) %collective-permute-start.24) | collective-permute-done | bytes 131104 | tf_op jit(solution)/shard_map/ppermute | solution.py:766
  178.2 2.9 %collective-permute-done.25 = bf16[1,128,256]{2,1,0:T(8,128)(2,1)S(1)} collective-permute-done((bf16[1,128,256]{2,1,0:T(8,128)(2,1)S(1)}, bf16[1,128,256]{2,1,0:T(8,128)(2,1)S(1)}, u32[]{:S(2)}, u32[]{:S(2)}) %collective-permute-start.25) | collective-permute-done | bytes 65568 | tf_op jit(solution)/shard_map/ppermute | solution.py:766
  181.3 6.5 %all_gather.4.s_ref = bf16[4,256,256]{2,1,0:T(8,128)(2,1)S(1)} all-gather(bf16[1,256,256]{2,1,0:T(8,128)(2,1)S(1)} %fusion.1), channel_id=1, replica_groups=mesh['slab'=8,'chan'=4] {'chan'}, dimensions={0}, use_global_device_ids=true | all-gather | bytes 655360 | tf_op jit(solution)/shard_map/all_gather | solution.py:852
  190.0 7.1 %unmix.1 = bf16[256,256]{1,0:T(8,128)(2,1)S(1)} custom-call(bf16[4,256,256]{2,1,0:T(8,128)(2,1)S(1)} %all_gather.4.s_ref, bf16[2,8,32,4096]{3,2,1,0:T(8,128)(2,1)S(1)} %copy-done.4, bf16[128,2048]{1,0:T(8,128)(2,1)S(1)} %copy-done.9, bf16[2048,128]{1,0:T(8,128)(2,1)S(1)} %copy-done.8), custom_call_target="tpu_custom_call" | custom-call | flops 8388608 | bytes 4194304 | tf_op jit(solution)/shard_map/unmix/pallas_call | solution.py:736
  198.3 5.6 %collective-permute-done.26 = bf16[1,128,256]{2,1,0:T(8,128)(2,1)S(1)} collective-permute-done((bf16[1,128,256]{2,1,0:T(8,128)(2,1)S(1)}, bf16[1,128,256]{2,1,0:T(8,128)(2,1)S(1)}, u32[]{:S(2)}, u32[]{:S(2)}) %collective-permute-start.26) | collective-permute-done | bytes 65568 | tf_op jit(solution)/shard_map/ppermute | solution.py:766
  206.4 4.3 %collective-permute-done.27 = bf16[2,128,256]{2,1,0:T(8,128)(2,1)S(1)} collective-permute-done((bf16[2,128,256]{2,1,0:T(8,128)(2,1)S(1)}, bf16[2,128,256]{2,1,0:T(8,128)(2,1)S(1)}, u32[]{:S(2)}, u32[]{:S(2)}) %collective-permute-start.27) | collective-permute-done | bytes 131104 | tf_op jit(solution)/shard_map/ppermute | solution.py:766
  212.8 4.9 %collective-permute-done.28.refs_1_ = bf16[4,128,256]{2,1,0:T(8,128)(2,1)S(1)} collective-permute-done((bf16[4,128,256]{2,1,0:T(8,128)(2,1)S(1)}, bf16[4,128,256]{2,1,0:T(8,128)(2,1)S(1)}, u32[]{:S(2)}, u32[]{:S(2)}) %collective-permute-start.28) | collective-permute-done | bytes 262176 | tf_op jit(solution)/shard_map/ppermute | solution.py:766
  219.2 4.0 %to_columns.3.q_ref = bf16[256,1024]{1,0:T(8,128)(2,1)S(1)} custom-call(s32[8,1,256]{2,1,0:T(1,128)S(1)} %broadcast_select_fusion.slots_ref, bf16[4,128,256]{2,1,0:T(8,128)(2,1)S(1)} %pad_maximum_fusion.2.refs_0_, bf16[4,128,256]{2,1,0:T(8,128)(2,1)S(1)} %collective-permute-done.28.refs_1_, bf16[4,128,256]{2,1,0:T(8,128)(2,1)S(1)} %pad_maximum_fusion.3.refs_2_, ...), custom_call_target="tpu_custom_call" | custom-call | tf_op jit(solution)/shard_map/to_columns/pallas_call | solution.py:602
  224.0 26.2 %finish.1 = bf16[8,32,256,256]{3,2,1,0:T(8,128)(2,1)} custom-call(bf16[256,1024]{1,0:T(8,128)(2,1)} %copy-done.7, bf16[8,32,256,256]{3,2,1,0:T(8,128)(2,1)} %get-tuple-element.23.g_ref, f32[8]{0:T(128)} %get-tuple-element.36.gain_ref, bf16[4,256,256]{2,1,0:T(8,128)(2,1)} %constant.124.clone.refs_11_.bd_ref, ...), custom_call_target="tpu_custom_call" | custom-call | flops 8589934592 | bytes 33554432 | tf_op jit(solution)/shard_map/finish/pallas_call | solution.py:437
  (144 shorter events, 66.2 us)
Async XLA Ops:
  0.7 31.5 %collective-permute-start.3 = (bf16[32,64,256]{2,1,0:T(8,128)(2,1)}, bf16[32,64,256]{2,1,0:T(8,128)(2,1)}, u32[]{:S(2)}, u32[]{:S(2)}) collective-permute-start(bf16[32,64,256]{2,1,0:T(8,128)(2,1)} %refs_2_.1), channel_id=1, source_target_pairs={{0,2},{1,3},{2,0},{3,1},{4,6},{5,7},{6,4},{7,5},{8,10},{9,11},{10,... | collective-permute-start | bytes 3145736 | tf_op jit(solution)/shard_map/ppermute | solution.py:766
  11.9 20.3 %collective-permute-start.2 = (bf16[32,1024]{1,0:T(8,128)(2,1)S(1)}, bf16[32,1024]{1,0:T(8,128)(2,1)S(1)}, u32[]{:S(2)}, u32[]{:S(2)}) collective-permute-start(bf16[32,1024]{1,0:T(8,128)(2,1)S(1)} %forced.1.refs_0_), channel_id=1, source_target_pairs={{0,3},{1,2},{2,1},{3,0},{4,7},{5,6},{6,5},{7,4},{8,11},{9,10},{10,... | collective-permute-start | bytes 196616 | tf_op jit(solution)/shard_map/ppermute | solution.py:766
  12.0 20.2 %collective-permute-start.1 = (bf16[32,1024]{1,0:T(8,128)(2,1)S(1)}, bf16[32,1024]{1,0:T(8,128)(2,1)S(1)}, u32[]{:S(2)}, u32[]{:S(2)}) collective-permute-start(bf16[32,1024]{1,0:T(8,128)(2,1)S(1)} %forced.1.refs_0_), channel_id=1, source_target_pairs={{0,2},{1,3},{2,0},{3,1},{4,6},{5,7},{6,4},{7,5},{8,10},{9,11},{10,... | collective-permute-start | bytes 196616 | tf_op jit(solution)/shard_map/ppermute | solution.py:766
  13.2 19.0 %collective-permute-start = (bf16[32,1024]{1,0:T(8,128)(2,1)S(1)}, bf16[32,1024]{1,0:T(8,128)(2,1)S(1)}, u32[]{:S(2)}, u32[]{:S(2)}) collective-permute-start(bf16[32,1024]{1,0:T(8,128)(2,1)S(1)} %forced.1.refs_0_), channel_id=1, source_target_pairs={{0,1},{1,0},{2,3},{3,2},{4,5},{5,4},{6,7},{7,6},{8,9},{9,8},{10,11... | collective-permute-start | bytes 196616 | tf_op jit(solution)/shard_map/ppermute | solution.py:766
  36.1 8.3 %collective-permute-start.4 = (bf16[4,128,256]{2,1,0:T(8,128)(2,1)S(1)}, bf16[4,128,256]{2,1,0:T(8,128)(2,1)S(1)}, u32[]{:S(2)}, u32[]{:S(2)}) collective-permute-start(bf16[4,128,256]{2,1,0:T(8,128)(2,1)S(1)} %get-tuple-element.14), channel_id=1, source_target_pairs={{0,4},{4,0},{8,12},{12,8},{16,20},{20,16},{24,28},{28,24},{1,5},{5... | collective-permute-start | bytes 786440 | tf_op jit(solution)/shard_map/ppermute | solution.py:766
  37.6 8.4 %collective-permute-start.7 = (bf16[4,128,256]{2,1,0:T(8,128)(2,1)S(1)}, bf16[4,128,256]{2,1,0:T(8,128)(2,1)S(1)}, u32[]{:S(2)}, u32[]{:S(2)}) collective-permute-start(bf16[4,128,256]{2,1,0:T(8,128)(2,1)S(1)} %get-tuple-element.16), channel_id=1, source_target_pairs={{0,8},{4,12},{8,0},{12,4},{16,24},{20,28},{24,16},{28,20},{1,9},{5... | collective-permute-start | bytes 786440 | tf_op jit(solution)/shard_map/ppermute | solution.py:766
  44.4 6.4 %collective-permute-start.5 = (bf16[2,128,256]{2,1,0:T(8,128)(2,1)S(1)}, bf16[2,128,256]{2,1,0:T(8,128)(2,1)S(1)}, u32[]{:S(2)}, u32[]{:S(2)}) collective-permute-start(bf16[2,128,256]{2,1,0:T(8,128)(2,1)S(1)} %split.81), channel_id=1, source_target_pairs={{0,8},{4,12},{8,0},{12,4},{16,24},{20,28},{24,16},{28,20},{1,9},{5... | collective-permute-start | bytes 393224 | tf_op jit(solution)/shard_map/ppermute | solution.py:766
  46.2 9.5 %collective-permute-start.8 = (bf16[2,128,256]{2,1,0:T(8,128)(2,1)S(1)}, bf16[2,128,256]{2,1,0:T(8,128)(2,1)S(1)}, u32[]{:S(2)}, u32[]{:S(2)}) collective-permute-start(bf16[2,128,256]{2,1,0:T(8,128)(2,1)S(1)} %split.85), channel_id=1, source_target_pairs={{0,16},{4,20},{8,24},{12,28},{16,0},{20,4},{24,8},{28,12},{1,17},{... | collective-permute-start | bytes 393224 | tf_op jit(solution)/shard_map/ppermute | solution.py:766
  50.9 6.4 %collective-permute-start.6 = (bf16[1,128,256]{2,1,0:T(8,128)(2,1)S(1)}, bf16[1,128,256]{2,1,0:T(8,128)(2,1)S(1)}, u32[]{:S(2)}, u32[]{:S(2)}) collective-permute-start(bf16[1,128,256]{2,1,0:T(8,128)(2,1)S(1)} %get-tuple-element.34), channel_id=1, source_target_pairs={{0,16},{4,20},{8,24},{12,28},{16,0},{20,4},{24,8},{28,12},{1,17},{... | collective-permute-start | bytes 196616 | tf_op jit(solution)/shard_map/ppermute | solution.py:766
  70.5 33.7 %collective-permute-start.18 = (bf16[32,64,256]{2,1,0:T(8,128)(2,1)S(1)}, bf16[32,64,256]{2,1,0:T(8,128)(2,1)}, u32[]{:S(2)}, u32[]{:S(2)}) collective-permute-start(bf16[32,64,256]{2,1,0:T(8,128)(2,1)S(1)} %copy-done.11), channel_id=1, source_target_pairs={{0,1},{1,0},{2,3},{3,2},{4,5},{5,4},{6,7},{7,6},{8,9},{9,8},{10,11... | collective-permute-start | bytes 3145736 | tf_op jit(solution)/shard_map/ppermute | solution.py:766
  70.5 33.7 %collective-permute-start.19 = (bf16[32,64,256]{2,1,0:T(8,128)(2,1)}, bf16[32,64,256]{2,1,0:T(8,128)(2,1)}, u32[]{:S(2)}, u32[]{:S(2)}) collective-permute-start(bf16[32,64,256]{2,1,0:T(8,128)(2,1)} %collective-permute-done.3.refs_4_.refs_3_), channel_id=1, source_target_pairs={{0,1},{1,0},{2,3},{3,2},{4,5},{5,4},{6,7},{7,6},{8,9},{9,8},{10,11... | collective-permute-start | bytes 3145736 | tf_op jit(solution)/shard_map/ppermute | solution.py:766
  77.3 9.1 %collective-permute-start.12 = (bf16[1,128,256]{2,1,0:T(8,128)(2,1)S(1)}, bf16[1,128,256]{2,1,0:T(8,128)(2,1)S(1)}, u32[]{:S(2)}, u32[]{:S(2)}) collective-permute-start(bf16[1,128,256]{2,1,0:T(8,128)(2,1)S(1)} %get-tuple-element.31), channel_id=1, source_target_pairs={{0,16},{4,20},{8,24},{12,28},{16,0},{20,4},{24,8},{28,12},{1,17},{... | collective-permute-start | bytes 196616 | tf_op jit(solution)/shard_map/ppermute | solution.py:766
  79.4 13.5 %collective-permute-start.16 = (bf16[2,128,256]{2,1,0:T(8,128)(2,1)S(1)}, bf16[2,128,256]{2,1,0:T(8,128)(2,1)S(1)}, u32[]{:S(2)}, u32[]{:S(2)}) collective-permute-start(bf16[2,128,256]{2,1,0:T(8,128)(2,1)S(1)} %pad_maximum_fusion.5), channel_id=1, source_target_pairs={{0,16},{4,20},{8,24},{12,28},{16,0},{20,4},{24,8},{28,12},{1,17},{... | collective-permute-start | bytes 393224 | tf_op jit(solution)/shard_map/ppermute | solution.py:766
  86.4 6.4 %collective-permute-start.13 = (bf16[2,128,256]{2,1,0:T(8,128)(2,1)S(1)}, bf16[2,128,256]{2,1,0:T(8,128)(2,1)S(1)}, u32[]{:S(2)}, u32[]{:S(2)}) collective-permute-start(bf16[2,128,256]{2,1,0:T(8,128)(2,1)S(1)} %pad_maximum_fusion.4), channel_id=1, source_target_pairs={{0,8},{4,12},{8,0},{12,4},{16,24},{20,28},{24,16},{28,20},{1,9},{5... | collective-permute-start | bytes 393224 | tf_op jit(solution)/shard_map/ppermute | solution.py:766
  92.8 6.4 %collective-permute-start.14 = (bf16[4,128,256]{2,1,0:T(8,128)(2,1)S(1)}, bf16[4,128,256]{2,1,0:T(8,128)(2,1)S(1)}, u32[]{:S(2)}, u32[]{:S(2)}) collective-permute-start(bf16[4,128,256]{2,1,0:T(8,128)(2,1)S(1)} %pad_maximum_fusion.refs_0_), channel_id=1, source_target_pairs={{0,4},{4,0},{8,12},{12,8},{16,20},{20,16},{24,28},{28,24},{1,5},{5... | collective-permute-start | bytes 786440 | tf_op jit(solution)/shard_map/ppermute | solution.py:766
  92.9 6.4 %collective-permute-start.17 = (bf16[4,128,256]{2,1,0:T(8,128)(2,1)S(1)}, bf16[4,128,256]{2,1,0:T(8,128)(2,1)S(1)}, u32[]{:S(2)}, u32[]{:S(2)}) collective-permute-start(bf16[4,128,256]{2,1,0:T(8,128)(2,1)S(1)} %pad_maximum_fusion.1.refs_2_), channel_id=1, source_target_pairs={{0,8},{4,12},{8,0},{12,4},{16,24},{20,28},{24,16},{28,20},{1,9},{5... | collective-permute-start | bytes 786440 | tf_op jit(solution)/shard_map/ppermute | solution.py:766
  160.3 6.4 %collective-permute-start.20 = (bf16[4,128,256]{2,1,0:T(8,128)(2,1)S(1)}, bf16[4,128,256]{2,1,0:T(8,128)(2,1)S(1)}, u32[]{:S(2)}, u32[]{:S(2)}) collective-permute-start(bf16[4,128,256]{2,1,0:T(8,128)(2,1)S(1)} %get-tuple-element.20), channel_id=1, source_target_pairs={{0,4},{4,0},{8,12},{12,8},{16,20},{20,16},{24,28},{28,24},{1,5},{5... | collective-permute-start | bytes 786440 | tf_op jit(solution)/shard_map/ppermute | solution.py:766
  162.5 7.8 %collective-permute-start.23 = (bf16[4,128,256]{2,1,0:T(8,128)(2,1)S(1)}, bf16[4,128,256]{2,1,0:T(8,128)(2,1)S(1)}, u32[]{:S(2)}, u32[]{:S(2)}) collective-permute-start(bf16[4,128,256]{2,1,0:T(8,128)(2,1)S(1)} %get-tuple-element.22), channel_id=1, source_target_pairs={{0,8},{4,12},{8,0},{12,4},{16,24},{20,28},{24,16},{28,20},{1,9},{5... | collective-permute-start | bytes 786440 | tf_op jit(solution)/shard_map/ppermute | solution.py:766
  197.1 6.7 %collective-permute-start.26 = (bf16[1,128,256]{2,1,0:T(8,128)(2,1)S(1)}, bf16[1,128,256]{2,1,0:T(8,128)(2,1)S(1)}, u32[]{:S(2)}, u32[]{:S(2)}) collective-permute-start(bf16[1,128,256]{2,1,0:T(8,128)(2,1)S(1)} %get-tuple-element.29), channel_id=1, source_target_pairs={{0,16},{4,20},{8,24},{12,28},{16,0},{20,4},{24,8},{28,12},{1,17},{... | collective-permute-start | bytes 196616 | tf_op jit(solution)/shard_map/ppermute | solution.py:766
  197.2 6.7 %collective-permute-start.29 = (bf16[1,128,256]{2,1,0:T(8,128)(2,1)S(1)}, bf16[1,128,256]{2,1,0:T(8,128)(2,1)S(1)}, u32[]{:S(2)}, u32[]{:S(2)}) collective-permute-start(bf16[1,128,256]{2,1,0:T(8,128)(2,1)S(1)} %get-tuple-element.28), channel_id=1, source_target_pairs={{0,4},{4,0},{8,12},{12,8},{16,20},{20,16},{24,28},{28,24},{1,5},{5... | collective-permute-start | bytes 196616 | tf_op jit(solution)/shard_map/ppermute | solution.py:766
  203.8 6.9 %collective-permute-start.27 = (bf16[2,128,256]{2,1,0:T(8,128)(2,1)S(1)}, bf16[2,128,256]{2,1,0:T(8,128)(2,1)S(1)}, u32[]{:S(2)}, u32[]{:S(2)}) collective-permute-start(bf16[2,128,256]{2,1,0:T(8,128)(2,1)S(1)} %pad_maximum_fusion.6), channel_id=1, source_target_pairs={{0,8},{4,12},{8,0},{12,4},{16,24},{20,28},{24,16},{28,20},{1,9},{5... | collective-permute-start | bytes 393224 | tf_op jit(solution)/shard_map/ppermute | solution.py:766
  203.9 8.8 %collective-permute-start.30 = (bf16[2,128,256]{2,1,0:T(8,128)(2,1)S(1)}, bf16[2,128,256]{2,1,0:T(8,128)(2,1)S(1)}, u32[]{:S(2)}, u32[]{:S(2)}) collective-permute-start(bf16[2,128,256]{2,1,0:T(8,128)(2,1)S(1)} %pad_maximum_fusion.7), channel_id=1, source_target_pairs={{0,16},{4,20},{8,24},{12,28},{16,0},{20,4},{24,8},{28,12},{1,17},{... | collective-permute-start | bytes 393224 | tf_op jit(solution)/shard_map/ppermute | solution.py:766
  210.8 7.0 %collective-permute-start.28 = (bf16[4,128,256]{2,1,0:T(8,128)(2,1)S(1)}, bf16[4,128,256]{2,1,0:T(8,128)(2,1)S(1)}, u32[]{:S(2)}, u32[]{:S(2)}) collective-permute-start(bf16[4,128,256]{2,1,0:T(8,128)(2,1)S(1)} %pad_maximum_fusion.2.refs_0_), channel_id=1, source_target_pairs={{0,4},{4,0},{8,12},{12,8},{16,20},{20,16},{24,28},{28,24},{1,5},{5... | collective-permute-start | bytes 786440 | tf_op jit(solution)/shard_map/ppermute | solution.py:766
  212.7 6.4 %collective-permute-start.31 = (bf16[4,128,256]{2,1,0:T(8,128)(2,1)S(1)}, bf16[4,128,256]{2,1,0:T(8,128)(2,1)S(1)}, u32[]{:S(2)}, u32[]{:S(2)}) collective-permute-start(bf16[4,128,256]{2,1,0:T(8,128)(2,1)S(1)} %pad_maximum_fusion.3.refs_2_), channel_id=1, source_target_pairs={{0,8},{4,12},{8,0},{12,4},{16,24},{20,28},{24,16},{28,20},{1,9},{5... | collective-permute-start | bytes 786440 | tf_op jit(solution)/shard_map/ppermute | solution.py:766
  (27 other events, 602.0 us)

commit v2 on v1

--- a/solution.py
+++ b/solution.py
@@ -174,7 +174,7 @@
         functools.partial(analyse_kernel, factor),
         in_specs=[anywhere(), resident(), resident(), anywhere(), resident()],
         out_specs=resident(),
-        out_shape=jax.ShapeDtypeStruct((channels * KXY, width), BF16),
+        out_shape=pltpu.VMEM((channels * KXY, width), BF16),
         scratch_shapes=[
             pltpu.VMEM((channels * KXY, width), F32),
             pltpu.VMEM((channels * KXY, 2 * HALF), BF16),
@@ -221,7 +221,7 @@
             pltpu.VMEM(tz.shape, BF16),
             pltpu.SemaphoreType.DMA,
         ],
-        compiler_params=pltpu.CompilerParams(vmem_limit_bytes=SMALL),
+        compiler_params=pltpu.CompilerParams(vmem_limit_bytes=LARGE),
         name="forced",
     )(forcing, rt, tx, tz, phase)
 
@@ -352,7 +352,7 @@
         out_shape=[
             jax.ShapeDtypeStruct(kept.shape, BF16),
             jax.ShapeDtypeStruct(kept.shape, BF16),
-            jax.ShapeDtypeStruct((channels * KXY, width), BF16),
+            pltpu.VMEM((channels * KXY, width), BF16),
         ],
         scratch_shapes=[
             pltpu.VMEM((channels * KXY, width), F32),

time: 251 us -> 249 us (level)
  local copies, waits for them, and re-layouts: 18.7 us -> 13.3 us
  Pallas kernels: 124 us -> 127 us
    unnamed x38 -> x28, local copies, waits for them, and re-layouts: 12.5 us -> 6.05 us
    pallas_call x1, Pallas kernels: 2.27 us -> 5.23 us  [analyse_forced(): pl.pallas_call(functools.partial(forced_kernel, factor), in_specs=[reside...]
  transfers between devices with their start and end apart: 32 -> 32, of which waited for: 22 -> 22; matrix products, arithmetic and copies ran while one was open for 4% -> 5% of each run, Pallas kernels for 10% -> 11%
where the time goes in v2:
time: 249 us; the launch traced here: 248 us
  Pallas kernels  127 us (51%)
  waiting for transfers between devices  65 us (26%)
  starting transfers between devices  30.3 us (12%)
  local copies, waits for them, and re-layouts  13.3 us (5%)
  blocking collectives  6.51 us (3%)
  other arithmetic  4.83 us (2%)
    ppermute x32, waiting for transfers between devices, exchange(): return lax.ppermute(value, axis, [(k, k ^ offset) for k in range(size)])  65 us
    pallas_call x1, Pallas kernels, middle(): pl.pallas_call(functools.partial(middle_kernel, factor, parts), in_specs=...  53.3 us
    ppermute x32, starting transfers between devices, exchange(): return lax.ppermute(value, axis, [(k, k ^ offset) for k in range(size)])  30.3 us
    pallas_call x1, Pallas kernels, finish(): pl.pallas_call(finish_kernel, in_specs=[resident(), anywhere(), scalars()...  25.9 us
    pallas_call x1, Pallas kernels, analyse(): pl.pallas_call(functools.partial(analyse_kernel, factor), in_specs=[anywh...  16.3 us
    pallas_call x2, Pallas kernels, to_columns(): pl.pallas_call(functools.partial(to_columns_kernel, places), out_shape=ja...  7.95 us
    pallas_call x1, Pallas kernels, unmix(): pl.pallas_call(unmix_kernel, out_shape=jax.ShapeDtypeStruct((2 * KZ * cha...  7.23 us
    all_gather x1, blocking collectives, per_device(): everyone = lax.all_gather(sums, 'chan', axis=0)  6.51 us
  transfers between devices with their start and end apart: 32, of which 22 were waited for; matrix products, arithmetic and copies ran while one was open for 5% of the time, Pallas kernels for 11%

profile of v2, /device:TPU:0, one launch (start us, length us, event | category | flops | bytes accessed | tf_op | source)
XLA Modules:
  0.0 248.1 jit_solution(10381971396174211216)
XLA Ops:
  0.7 3.0 %collective-permute-start.3 = (bf16[32,64,256]{2,1,0:T(8,128)(2,1)}, bf16[32,64,256]{2,1,0:T(8,128)(2,1)S(1)}, u32[]{:S(2)}, u32[]{:S(2)}) collective-permute-start(bf16[32,64,256]{2,1,0:T(8,128)(2,1)} %refs_2_.1), channel_id=1, source_target_pairs={{0,2},{1,3},{2,0},{3,1},{4,6},{5,7},{6,4},{7,5},{8,10},{9,11},{10,... | collective-permute-start | bytes 3145736 | tf_op jit(solution)/shard_map/ppermute | solution.py:766
  6.4 5.2 %forced.1.refs_0_ = bf16[32,1024]{1,0:T(8,128)(2,1)} custom-call(bf16[32,64,256]{2,1,0:T(8,128)(2,1)} %refs_2_.1, bf16[4,256,256]{2,1,0:T(8,128)(2,1)} %constant.123.clone.rt_ref.refs_10_, bf16[64,64]{1,0:T(8,128)(2,1)} %constant_dynamic-slice_fusion.1.tx_ref, bf16[8,256,1024]{2,1,0:T(8,128)(2,1)} %constant.127.clone.tz_hbm.refs_14_, ...), custom_call_target="tpu_custom_call" | custom-call | tf_op jit(solution)/shard_map/forced/pallas_call | solution.py:214
  14.9 16.3 %analyse.1.d_ref = bf16[256,1024]{1,0:T(8,128)(2,1)S(1)} custom-call(bf16[8,32,256,256]{3,2,1,0:T(8,128)(2,1)} %refs_1_.1, bf16[4,256,256]{2,1,0:T(8,128)(2,1)} %constant.123.clone.rt_ref.refs_10_, bf16[64,256]{1,0:T(8,128)(2,1)} %constant.125.clone.tx_ref.refs_12_, bf16[8,256,1024]{2,1,0:T(8,128)(2,1)} %constant.127.clone.tz_hbm.refs_14_, ...), custom_call_target="tpu_custom_call" | custom-call | flops 134217728 | bytes 2097152 | tf_op jit(solution)/shard_map/analyse/pallas_call | solution.py:173
  31.3 2.8 %to_slots.2 = (bf16[4,128,256]{2,1,0:T(8,128)(2,1)S(1)}, bf16[4,128,256]{2,1,0:T(8,128)(2,1)S(1)}, bf16[4,128,256]{2,1,0:T(8,128)(2,1)S(1)}, bf16[4,128,256]{2,1,0:T(8,128)(2,1)S(1)}) custom-call(s32[8,1,256]{2,1,0:T(1,128)S(1)} %broadcast_select_fusion.slots_ref, bf16[256,1024]{1,0:T(8,128)(2,1)S(1)} %analyse.1.d_ref, bf16[32,1024]{1,0:T(8,128)(2,1)S(1)} %copy-done.9, ...), custom_call_target="tpu_custom_call" | custom-call | tf_op jit(solution)/shard_map/to_slots/pallas_call | solution.py:552
  37.2 5.1 %collective-permute-done.4 = bf16[4,128,256]{2,1,0:T(8,128)(2,1)S(1)} collective-permute-done((bf16[4,128,256]{2,1,0:T(8,128)(2,1)S(1)}, bf16[4,128,256]{2,1,0:T(8,128)(2,1)S(1)}, u32[]{:S(2)}, u32[]{:S(2)}) %collective-permute-start.4) | collective-permute-done | bytes 262176 | tf_op jit(solution)/shard_map/ppermute | solution.py:766
  55.3 2.8 %collective-permute-done.9.d_ref = bf16[1,128,256]{2,1,0:T(8,128)(2,1)S(1)} collective-permute-done((bf16[1,128,256]{2,1,0:T(8,128)(2,1)S(1)}, bf16[1,128,256]{2,1,0:T(8,128)(2,1)S(1)}, u32[]{:S(2)}, u32[]{:S(2)}) %collective-permute-start.9) | collective-permute-done | bytes 65568 | tf_op jit(solution)/shard_map/ppermute | solution.py:766
  60.3 4.6 %mix.1 = bf16[4,2,8,4096]{3,2,1,0:T(8,128)(2,1)S(1)} custom-call(bf16[1,128,256]{2,1,0:T(8,128)(2,1)S(1)} %get-tuple-element.35.a_ref, bf16[1,128,256]{2,1,0:T(8,128)(2,1)S(1)} %collective-permute-done.6.b_ref, bf16[1,128,256]{2,1,0:T(8,128)(2,1)S(1)} %get-tuple-element.33.c_ref, bf16[1,128,256]{2,1,0:T(8,128)(2,1)S(1)} %collective-permute-done.9.d_ref, ...), custom_call_target="tpu_custom_call" | custom-call | flops 8388608 | bytes 4194304 | tf_op jit(solution)/shard_map/mix/pallas_call | solution.py:661
  68.8 3.4 %collective-permute-done.11 = bf16[1,2,8,4096]{3,2,1,0:T(8,128)(2,1)S(1)} collective-permute-done((bf16[1,2,8,4096]{3,2,1,0:T(8,128)(2,1)S(1)}, bf16[1,2,8,4096]{3,2,1,0:T(8,128)(2,1)S(1)}, u32[]{:S(2)}, u32[]{:S(2)}) %collective-permute-start.11) | collective-permute-done | bytes 131104 | tf_op jit(solution)/shard_map/ppermute | solution.py:766
  78.1 6.1 %collective-permute-done.12 = bf16[1,128,256]{2,1,0:T(8,128)(2,1)S(1)} collective-permute-done((bf16[1,128,256]{2,1,0:T(8,128)(2,1)S(1)}, bf16[1,128,256]{2,1,0:T(8,128)(2,1)S(1)}, u32[]{:S(2)}, u32[]{:S(2)}) %collective-permute-start.12) | collective-permute-done | bytes 65568 | tf_op jit(solution)/shard_map/ppermute | solution.py:766
  86.4 4.3 %collective-permute-done.13 = bf16[2,128,256]{2,1,0:T(8,128)(2,1)S(1)} collective-permute-done((bf16[2,128,256]{2,1,0:T(8,128)(2,1)S(1)}, bf16[2,128,256]{2,1,0:T(8,128)(2,1)S(1)}, u32[]{:S(2)}, u32[]{:S(2)}) %collective-permute-start.13) | collective-permute-done | bytes 131104 | tf_op jit(solution)/shard_map/ppermute | solution.py:766
  97.3 4.0 %to_columns.2.refs_0_ = bf16[256,1024]{1,0:T(8,128)(2,1)S(1)} custom-call(s32[8,1,256]{2,1,0:T(1,128)S(1)} %broadcast_select_fusion.slots_ref, bf16[4,128,256]{2,1,0:T(8,128)(2,1)S(1)} %pad_maximum_fusion.refs_0_, bf16[4,128,256]{2,1,0:T(8,128)(2,1)S(1)} %collective-permute-done.14.refs_1_, bf16[4,128,256]{2,1,0:T(8,128)(2,1)S(1)} %pad_maximum_fusion.1.refs_2_, ...), custom_call_target="tpu_custom_call" | custom-call | tf_op jit(solution)/shard_map/to_columns/pallas_call | solution.py:602
  102.1 53.3 %middle.1 = (bf16[8,32,256,256]{3,2,1,0:T(8,128)(2,1)}, bf16[8,32,256,256]{3,2,1,0:T(8,128)(2,1)}, bf16[256,1024]{1,0:T(8,128)(2,1)S(1)}) custom-call(bf16[256,1024]{1,0:T(8,128)(2,1)} %copy-done.8, bf16[8,32,256,256]{3,2,1,0:T(8,128)(2,1)} %refs_1_.1, bf16[32,64,256]{2,1,0:T(8,128)(2,1)} %refs_2_.1, bf16[32,64,256]{2,1,0:T(8,128)(2,1)} %copy-done.7, ...), custom_call_target="tpu_custom_call" | custom-call | flops 17179869184 | bytes 33554432 | tf_op jit(solution)/shard_map/middle/pallas_call | solution.py:348
  155.4 2.7 %to_slots.3 = (bf16[4,128,256]{2,1,0:T(8,128)(2,1)S(1)}, bf16[4,128,256]{2,1,0:T(8,128)(2,1)S(1)}, bf16[4,128,256]{2,1,0:T(8,128)(2,1)S(1)}, bf16[4,128,256]{2,1,0:T(8,128)(2,1)S(1)}) custom-call(s32[8,1,256]{2,1,0:T(1,128)S(1)} %broadcast_select_fusion.slots_ref, bf16[256,1024]{1,0:T(8,128)(2,1)S(1)} %get-tuple-element.18.d_ref), custom_call_target="tpu_custom_call" | custom-call | tf_op jit(solution)/shard_map/to_slots/pallas_call | solution.py:552
  160.4 4.1 %collective-permute-done.20 = bf16[4,128,256]{2,1,0:T(8,128)(2,1)S(1)} collective-permute-done((bf16[4,128,256]{2,1,0:T(8,128)(2,1)S(1)}, bf16[4,128,256]{2,1,0:T(8,128)(2,1)S(1)}, u32[]{:S(2)}, u32[]{:S(2)}) %collective-permute-start.20) | collective-permute-done | bytes 262176 | tf_op jit(solution)/shard_map/ppermute | solution.py:766
  164.7 3.4 %collective-permute-done.23 = bf16[4,128,256]{2,1,0:T(8,128)(2,1)S(1)} collective-permute-done((bf16[4,128,256]{2,1,0:T(8,128)(2,1)S(1)}, bf16[4,128,256]{2,1,0:T(8,128)(2,1)S(1)}, u32[]{:S(2)}, u32[]{:S(2)}) %collective-permute-start.23) | collective-permute-done | bytes 262176 | tf_op jit(solution)/shard_map/ppermute | solution.py:766
  171.4 3.2 %collective-permute-done.24 = bf16[2,128,256]{2,1,0:T(8,128)(2,1)S(1)} collective-permute-done((bf16[2,128,256]{2,1,0:T(8,128)(2,1)S(1)}, bf16[2,128,256]{2,1,0:T(8,128)(2,1)S(1)}, u32[]{:S(2)}, u32[]{:S(2)}) %collective-permute-start.24) | collective-permute-done | bytes 131104 | tf_op jit(solution)/shard_map/ppermute | solution.py:766
  176.1 2.8 %collective-permute-done.25 = bf16[1,128,256]{2,1,0:T(8,128)(2,1)S(1)} collective-permute-done((bf16[1,128,256]{2,1,0:T(8,128)(2,1)S(1)}, bf16[1,128,256]{2,1,0:T(8,128)(2,1)S(1)}, u32[]{:S(2)}, u32[]{:S(2)}) %collective-permute-start.25) | collective-permute-done | bytes 65568 | tf_op jit(solution)/shard_map/ppermute | solution.py:766
  179.1 6.5 %all_gather.4.s_ref = bf16[4,256,256]{2,1,0:T(8,128)(2,1)S(1)} all-gather(bf16[1,256,256]{2,1,0:T(8,128)(2,1)S(1)} %fusion.1), channel_id=1, replica_groups=mesh['slab'=8,'chan'=4] {'chan'}, dimensions={0}, use_global_device_ids=true | all-gather | bytes 655360 | tf_op jit(solution)/shard_map/all_gather | solution.py:852
  187.8 7.2 %unmix.1 = bf16[256,256]{1,0:T(8,128)(2,1)S(1)} custom-call(bf16[4,256,256]{2,1,0:T(8,128)(2,1)S(1)} %all_gather.4.s_ref, bf16[2,8,32,4096]{3,2,1,0:T(8,128)(2,1)S(1)} %copy-done.3, bf16[128,2048]{1,0:T(8,128)(2,1)S(1)} %copy-done.6, bf16[2048,128]{1,0:T(8,128)(2,1)S(1)} %copy-done.5), custom_call_target="tpu_custom_call" | custom-call | flops 8388608 | bytes 4194304 | tf_op jit(solution)/shard_map/unmix/pallas_call | solution.py:736
  196.2 5.6 %collective-permute-done.26 = bf16[1,128,256]{2,1,0:T(8,128)(2,1)S(1)} collective-permute-done((bf16[1,128,256]{2,1,0:T(8,128)(2,1)S(1)}, bf16[1,128,256]{2,1,0:T(8,128)(2,1)S(1)}, u32[]{:S(2)}, u32[]{:S(2)}) %collective-permute-start.26) | collective-permute-done | bytes 65568 | tf_op jit(solution)/shard_map/ppermute | solution.py:766
  204.4 4.3 %collective-permute-done.27 = bf16[2,128,256]{2,1,0:T(8,128)(2,1)S(1)} collective-permute-done((bf16[2,128,256]{2,1,0:T(8,128)(2,1)S(1)}, bf16[2,128,256]{2,1,0:T(8,128)(2,1)S(1)}, u32[]{:S(2)}, u32[]{:S(2)}) %collective-permute-start.27) | collective-permute-done | bytes 131104 | tf_op jit(solution)/shard_map/ppermute | solution.py:766
  210.8 4.9 %collective-permute-done.28.refs_1_ = bf16[4,128,256]{2,1,0:T(8,128)(2,1)S(1)} collective-permute-done((bf16[4,128,256]{2,1,0:T(8,128)(2,1)S(1)}, bf16[4,128,256]{2,1,0:T(8,128)(2,1)S(1)}, u32[]{:S(2)}, u32[]{:S(2)}) %collective-permute-start.28) | collective-permute-done | bytes 262176 | tf_op jit(solution)/shard_map/ppermute | solution.py:766
  217.1 4.0 %to_columns.3.q_ref = bf16[256,1024]{1,0:T(8,128)(2,1)S(1)} custom-call(s32[8,1,256]{2,1,0:T(1,128)S(1)} %broadcast_select_fusion.slots_ref, bf16[4,128,256]{2,1,0:T(8,128)(2,1)S(1)} %pad_maximum_fusion.2.refs_0_, bf16[4,128,256]{2,1,0:T(8,128)(2,1)S(1)} %collective-permute-done.28.refs_1_, bf16[4,128,256]{2,1,0:T(8,128)(2,1)S(1)} %pad_maximum_fusion.3.refs_2_, ...), custom_call_target="tpu_custom_call" | custom-call | tf_op jit(solution)/shard_map/to_columns/pallas_call | solution.py:602
  221.9 25.9 %finish.1 = bf16[8,32,256,256]{3,2,1,0:T(8,128)(2,1)} custom-call(bf16[256,1024]{1,0:T(8,128)(2,1)} %copy-done.4, bf16[8,32,256,256]{3,2,1,0:T(8,128)(2,1)} %get-tuple-element.23.g_ref, f32[8]{0:T(128)} %get-tuple-element.36.gain_ref, bf16[4,256,256]{2,1,0:T(8,128)(2,1)} %constant.124.clone.refs_11_.bd_ref, ...), custom_call_target="tpu_custom_call" | custom-call | flops 8589934592 | bytes 33554432 | tf_op jit(solution)/shard_map/finish/pallas_call | solution.py:437
  (134 shorter events, 61.1 us)
Async XLA Ops:
  0.7 30.5 %collective-permute-start.3 = (bf16[32,64,256]{2,1,0:T(8,128)(2,1)}, bf16[32,64,256]{2,1,0:T(8,128)(2,1)S(1)}, u32[]{:S(2)}, u32[]{:S(2)}) collective-permute-start(bf16[32,64,256]{2,1,0:T(8,128)(2,1)} %refs_2_.1), channel_id=1, source_target_pairs={{0,2},{1,3},{2,0},{3,1},{4,6},{5,7},{6,4},{7,5},{8,10},{9,11},{10,... | collective-permute-start | bytes 3145736 | tf_op jit(solution)/shard_map/ppermute | solution.py:766
  11.6 19.6 %collective-permute-start.2 = (bf16[32,1024]{1,0:T(8,128)(2,1)}, bf16[32,1024]{1,0:T(8,128)(2,1)S(1)}, u32[]{:S(2)}, u32[]{:S(2)}) collective-permute-start(bf16[32,1024]{1,0:T(8,128)(2,1)} %forced.1.refs_0_), channel_id=1, source_target_pairs={{0,3},{1,2},{2,1},{3,0},{4,7},{5,6},{6,5},{7,4},{8,11},{9,10},{10,... | collective-permute-start | bytes 196616 | tf_op jit(solution)/shard_map/ppermute | solution.py:766
  11.7 19.5 %collective-permute-start.1 = (bf16[32,1024]{1,0:T(8,128)(2,1)}, bf16[32,1024]{1,0:T(8,128)(2,1)S(1)}, u32[]{:S(2)}, u32[]{:S(2)}) collective-permute-start(bf16[32,1024]{1,0:T(8,128)(2,1)} %forced.1.refs_0_), channel_id=1, source_target_pairs={{0,2},{1,3},{2,0},{3,1},{4,6},{5,7},{6,4},{7,5},{8,10},{9,11},{10,... | collective-permute-start | bytes 196616 | tf_op jit(solution)/shard_map/ppermute | solution.py:766
  12.9 18.3 %collective-permute-start = (bf16[32,1024]{1,0:T(8,128)(2,1)}, bf16[32,1024]{1,0:T(8,128)(2,1)S(1)}, u32[]{:S(2)}, u32[]{:S(2)}) collective-permute-start(bf16[32,1024]{1,0:T(8,128)(2,1)} %forced.1.refs_0_), channel_id=1, source_target_pairs={{0,1},{1,0},{2,3},{3,2},{4,5},{5,4},{6,7},{7,6},{8,9},{9,8},{10,11... | collective-permute-start | bytes 196616 | tf_op jit(solution)/shard_map/ppermute | solution.py:766
  34.1 8.3 %collective-permute-start.4 = (bf16[4,128,256]{2,1,0:T(8,128)(2,1)S(1)}, bf16[4,128,256]{2,1,0:T(8,128)(2,1)S(1)}, u32[]{:S(2)}, u32[]{:S(2)}) collective-permute-start(bf16[4,128,256]{2,1,0:T(8,128)(2,1)S(1)} %get-tuple-element.14), channel_id=1, source_target_pairs={{0,4},{4,0},{8,12},{12,8},{16,20},{20,16},{24,28},{28,24},{1,5},{5... | collective-permute-start | bytes 786440 | tf_op jit(solution)/shard_map/ppermute | solution.py:766
  35.7 8.4 %collective-permute-start.7 = (bf16[4,128,256]{2,1,0:T(8,128)(2,1)S(1)}, bf16[4,128,256]{2,1,0:T(8,128)(2,1)S(1)}, u32[]{:S(2)}, u32[]{:S(2)}) collective-permute-start(bf16[4,128,256]{2,1,0:T(8,128)(2,1)S(1)} %get-tuple-element.16), channel_id=1, source_target_pairs={{0,8},{4,12},{8,0},{12,4},{16,24},{20,28},{24,16},{28,20},{1,9},{5... | collective-permute-start | bytes 786440 | tf_op jit(solution)/shard_map/ppermute | solution.py:766
  42.4 6.4 %collective-permute-start.5 = (bf16[2,128,256]{2,1,0:T(8,128)(2,1)S(1)}, bf16[2,128,256]{2,1,0:T(8,128)(2,1)S(1)}, u32[]{:S(2)}, u32[]{:S(2)}) collective-permute-start(bf16[2,128,256]{2,1,0:T(8,128)(2,1)S(1)} %split.81), channel_id=1, source_target_pairs={{0,8},{4,12},{8,0},{12,4},{16,24},{20,28},{24,16},{28,20},{1,9},{5... | collective-permute-start | bytes 393224 | tf_op jit(solution)/shard_map/ppermute | solution.py:766
  44.2 9.5 %collective-permute-start.8 = (bf16[2,128,256]{2,1,0:T(8,128)(2,1)S(1)}, bf16[2,128,256]{2,1,0:T(8,128)(2,1)S(1)}, u32[]{:S(2)}, u32[]{:S(2)}) collective-permute-start(bf16[2,128,256]{2,1,0:T(8,128)(2,1)S(1)} %split.85), channel_id=1, source_target_pairs={{0,16},{4,20},{8,24},{12,28},{16,0},{20,4},{24,8},{28,12},{1,17},{... | collective-permute-start | bytes 393224 | tf_op jit(solution)/shard_map/ppermute | solution.py:766
  48.9 6.4 %collective-permute-start.6 = (bf16[1,128,256]{2,1,0:T(8,128)(2,1)S(1)}, bf16[1,128,256]{2,1,0:T(8,128)(2,1)S(1)}, u32[]{:S(2)}, u32[]{:S(2)}) collective-permute-start(bf16[1,128,256]{2,1,0:T(8,128)(2,1)S(1)} %get-tuple-element.34), channel_id=1, source_target_pairs={{0,16},{4,20},{8,24},{12,28},{16,0},{20,4},{24,8},{28,12},{1,17},{... | collective-permute-start | bytes 196616 | tf_op jit(solution)/shard_map/ppermute | solution.py:766
  68.3 33.8 %collective-permute-start.18 = (bf16[32,64,256]{2,1,0:T(8,128)(2,1)}, bf16[32,64,256]{2,1,0:T(8,128)(2,1)}, u32[]{:S(2)}, u32[]{:S(2)}) collective-permute-start(bf16[32,64,256]{2,1,0:T(8,128)(2,1)} %refs_2_.1), channel_id=1, source_target_pairs={{0,1},{1,0},{2,3},{3,2},{4,5},{5,4},{6,7},{7,6},{8,9},{9,8},{10,11... | collective-permute-start | bytes 3145736 | tf_op jit(solution)/shard_map/ppermute | solution.py:766
  68.3 33.8 %collective-permute-start.19 = (bf16[32,64,256]{2,1,0:T(8,128)(2,1)S(1)}, bf16[32,64,256]{2,1,0:T(8,128)(2,1)}, u32[]{:S(2)}, u32[]{:S(2)}) collective-permute-start(bf16[32,64,256]{2,1,0:T(8,128)(2,1)S(1)} %collective-permute-done.3.refs_4_.refs_3_), channel_id=1, source_target_pairs={{0,1},{1,0},{2,3},{3,2},{4,5},{5,4},{6,7},{7,6},{8,9},{9,8},{10,11... | collective-permute-start | bytes 3145736 | tf_op jit(solution)/shard_map/ppermute | solution.py:766
  75.1 9.1 %collective-permute-start.12 = (bf16[1,128,256]{2,1,0:T(8,128)(2,1)S(1)}, bf16[1,128,256]{2,1,0:T(8,128)(2,1)S(1)}, u32[]{:S(2)}, u32[]{:S(2)}) collective-permute-start(bf16[1,128,256]{2,1,0:T(8,128)(2,1)S(1)} %get-tuple-element.31), channel_id=1, source_target_pairs={{0,16},{4,20},{8,24},{12,28},{16,0},{20,4},{24,8},{28,12},{1,17},{... | collective-permute-start | bytes 196616 | tf_op jit(solution)/shard_map/ppermute | solution.py:766
  77.3 13.5 %collective-permute-start.16 = (bf16[2,128,256]{2,1,0:T(8,128)(2,1)S(1)}, bf16[2,128,256]{2,1,0:T(8,128)(2,1)S(1)}, u32[]{:S(2)}, u32[]{:S(2)}) collective-permute-start(bf16[2,128,256]{2,1,0:T(8,128)(2,1)S(1)} %pad_maximum_fusion.5), channel_id=1, source_target_pairs={{0,16},{4,20},{8,24},{12,28},{16,0},{20,4},{24,8},{28,12},{1,17},{... | collective-permute-start | bytes 393224 | tf_op jit(solution)/shard_map/ppermute | solution.py:766
  84.2 6.4 %collective-permute-start.13 = (bf16[2,128,256]{2,1,0:T(8,128)(2,1)S(1)}, bf16[2,128,256]{2,1,0:T(8,128)(2,1)S(1)}, u32[]{:S(2)}, u32[]{:S(2)}) collective-permute-start(bf16[2,128,256]{2,1,0:T(8,128)(2,1)S(1)} %pad_maximum_fusion.4), channel_id=1, source_target_pairs={{0,8},{4,12},{8,0},{12,4},{16,24},{20,28},{24,16},{28,20},{1,9},{5... | collective-permute-start | bytes 393224 | tf_op jit(solution)/shard_map/ppermute | solution.py:766
  90.7 6.4 %collective-permute-start.14 = (bf16[4,128,256]{2,1,0:T(8,128)(2,1)S(1)}, bf16[4,128,256]{2,1,0:T(8,128)(2,1)S(1)}, u32[]{:S(2)}, u32[]{:S(2)}) collective-permute-start(bf16[4,128,256]{2,1,0:T(8,128)(2,1)S(1)} %pad_maximum_fusion.refs_0_), channel_id=1, source_target_pairs={{0,4},{4,0},{8,12},{12,8},{16,20},{20,16},{24,28},{28,24},{1,5},{5... | collective-permute-start | bytes 786440 | tf_op jit(solution)/shard_map/ppermute | solution.py:766
  90.8 6.4 %collective-permute-start.17 = (bf16[4,128,256]{2,1,0:T(8,128)(2,1)S(1)}, bf16[4,128,256]{2,1,0:T(8,128)(2,1)S(1)}, u32[]{:S(2)}, u32[]{:S(2)}) collective-permute-start(bf16[4,128,256]{2,1,0:T(8,128)(2,1)S(1)} %pad_maximum_fusion.1.refs_2_), channel_id=1, source_target_pairs={{0,8},{4,12},{8,0},{12,4},{16,24},{20,28},{24,16},{28,20},{1,9},{5... | collective-permute-start | bytes 786440 | tf_op jit(solution)/shard_map/ppermute | solution.py:766
  158.1 6.4 %collective-permute-start.20 = (bf16[4,128,256]{2,1,0:T(8,128)(2,1)S(1)}, bf16[4,128,256]{2,1,0:T(8,128)(2,1)S(1)}, u32[]{:S(2)}, u32[]{:S(2)}) collective-permute-start(bf16[4,128,256]{2,1,0:T(8,128)(2,1)S(1)} %get-tuple-element.20), channel_id=1, source_target_pairs={{0,4},{4,0},{8,12},{12,8},{16,20},{20,16},{24,28},{28,24},{1,5},{5... | collective-permute-start | bytes 786440 | tf_op jit(solution)/shard_map/ppermute | solution.py:766
  160.3 7.8 %collective-permute-start.23 = (bf16[4,128,256]{2,1,0:T(8,128)(2,1)S(1)}, bf16[4,128,256]{2,1,0:T(8,128)(2,1)S(1)}, u32[]{:S(2)}, u32[]{:S(2)}) collective-permute-start(bf16[4,128,256]{2,1,0:T(8,128)(2,1)S(1)} %get-tuple-element.22), channel_id=1, source_target_pairs={{0,8},{4,12},{8,0},{12,4},{16,24},{20,28},{24,16},{28,20},{1,9},{5... | collective-permute-start | bytes 786440 | tf_op jit(solution)/shard_map/ppermute | solution.py:766
  195.0 6.7 %collective-permute-start.26 = (bf16[1,128,256]{2,1,0:T(8,128)(2,1)S(1)}, bf16[1,128,256]{2,1,0:T(8,128)(2,1)S(1)}, u32[]{:S(2)}, u32[]{:S(2)}) collective-permute-start(bf16[1,128,256]{2,1,0:T(8,128)(2,1)S(1)} %get-tuple-element.29), channel_id=1, source_target_pairs={{0,16},{4,20},{8,24},{12,28},{16,0},{20,4},{24,8},{28,12},{1,17},{... | collective-permute-start | bytes 196616 | tf_op jit(solution)/shard_map/ppermute | solution.py:766
  195.1 6.7 %collective-permute-start.29 = (bf16[1,128,256]{2,1,0:T(8,128)(2,1)S(1)}, bf16[1,128,256]{2,1,0:T(8,128)(2,1)S(1)}, u32[]{:S(2)}, u32[]{:S(2)}) collective-permute-start(bf16[1,128,256]{2,1,0:T(8,128)(2,1)S(1)} %get-tuple-element.28), channel_id=1, source_target_pairs={{0,4},{4,0},{8,12},{12,8},{16,20},{20,16},{24,28},{28,24},{1,5},{5... | collective-permute-start | bytes 196616 | tf_op jit(solution)/shard_map/ppermute | solution.py:766
  201.8 6.9 %collective-permute-start.27 = (bf16[2,128,256]{2,1,0:T(8,128)(2,1)S(1)}, bf16[2,128,256]{2,1,0:T(8,128)(2,1)S(1)}, u32[]{:S(2)}, u32[]{:S(2)}) collective-permute-start(bf16[2,128,256]{2,1,0:T(8,128)(2,1)S(1)} %pad_maximum_fusion.6), channel_id=1, source_target_pairs={{0,8},{4,12},{8,0},{12,4},{16,24},{20,28},{24,16},{28,20},{1,9},{5... | collective-permute-start | bytes 393224 | tf_op jit(solution)/shard_map/ppermute | solution.py:766
  201.9 8.8 %collective-permute-start.30 = (bf16[2,128,256]{2,1,0:T(8,128)(2,1)S(1)}, bf16[2,128,256]{2,1,0:T(8,128)(2,1)S(1)}, u32[]{:S(2)}, u32[]{:S(2)}) collective-permute-start(bf16[2,128,256]{2,1,0:T(8,128)(2,1)S(1)} %pad_maximum_fusion.7), channel_id=1, source_target_pairs={{0,16},{4,20},{8,24},{12,28},{16,0},{20,4},{24,8},{28,12},{1,17},{... | collective-permute-start | bytes 393224 | tf_op jit(solution)/shard_map/ppermute | solution.py:766
  208.7 7.0 %collective-permute-start.28 = (bf16[4,128,256]{2,1,0:T(8,128)(2,1)S(1)}, bf16[4,128,256]{2,1,0:T(8,128)(2,1)S(1)}, u32[]{:S(2)}, u32[]{:S(2)}) collective-permute-start(bf16[4,128,256]{2,1,0:T(8,128)(2,1)S(1)} %pad_maximum_fusion.2.refs_0_), channel_id=1, source_target_pairs={{0,4},{4,0},{8,12},{12,8},{16,20},{20,16},{24,28},{28,24},{1,5},{5... | collective-permute-start | bytes 786440 | tf_op jit(solution)/shard_map/ppermute | solution.py:766
  210.7 6.4 %collective-permute-start.31 = (bf16[4,128,256]{2,1,0:T(8,128)(2,1)S(1)}, bf16[4,128,256]{2,1,0:T(8,128)(2,1)S(1)}, u32[]{:S(2)}, u32[]{:S(2)}) collective-permute-start(bf16[4,128,256]{2,1,0:T(8,128)(2,1)S(1)} %pad_maximum_fusion.3.refs_2_), channel_id=1, source_target_pairs={{0,8},{4,12},{8,0},{12,4},{16,24},{20,28},{24,16},{28,20},{1,9},{5... | collective-permute-start | bytes 786440 | tf_op jit(solution)/shard_map/ppermute | solution.py:766
  (22 other events, 627.9 us)
